TPU v7x, 768 devices: a whole 4x8x12 slice. The times are simulated.
768 devices in a mesh: group: 96 (over z, x, core), member: 8 (over y).
Axes of the slice: x: 4, y: 8, z: 12, core: 2. Of those that a mesh axis runs over, the one named last changes fastest.
Arguments:
- edge_field: float32 [2, 3072, 1024], P(None, 'group', 'member'), may hold values from -6 to 6
- conductance: float32 [2, 3072, 1024], P(None, 'group', 'member'), may hold values from 0.5 to 4
- send_index: int32 [768, 96, 5], P(('group', 'member')), may hold values from 0 to 8191
- panel_source: int32 [3072, 128], P(('group', 'member')), may hold values from 0 to 479, as said below
- surface_field: float32 [3072, 128], P(('group', 'member')), may hold values from -6 to 6
- near_columns: int32 [3072, 4], P(('group', 'member')), may hold values from 0 to 31
- near_tiles: float32 [3072, 4, 128, 128], P(('group', 'member')), may hold values from -0.25 to 0.25
- far_columns: int32 [3072, 16], P(('group', 'member')), may hold values from 0 to 3071
- far_ranks: int32 [3072, 16], P(('group', 'member')), may hold values from 8 to 32
- far_coupling: float32 [3072, 16, 32, 32], P(('group', 'member')), may hold values from -1 to 1
- basis_left: float32 [3072, 128, 32], P(('group', 'member')), may hold values from -1 to 1
- basis_right: float32 [3072, 128, 32], P(('group', 'member')), may hold values from -0.5 to 0.5
Outputs:
- volume_out: float32 [2, 3072, 1024], P(None, 'group', 'member')
- surface_out: float32 [3072, 128], P(('group', 'member'))
Inputs may be any that keep to these rules, and one draw needn't show every extreme that they name: `panel_source`: on each device every one of the 480 trace slots is read by at least one of its panels.
All inputs are finite; a program needn't handle non-finite values.
Results may differ from a plain program's by a relative error of at most 0.000065.
Values sent between devices are 32-bit elements; how exact they have to be, the bound alone decides.
No kernel may reach another device: no remote copies, remote signals or barrier semaphores. Data moves between devices by JAX's collectives and lax.ppermute only.
A program may use at most 32 MiB of HBM per device.

v0:
```python
import jax
import jax.numpy as jnp
from jax import lax
from jax.sharding import PartitionSpec as P


def padded_2(cells, sides, width):
    for axis, dim in sides:
        count = lax.axis_size(axis)
        ends = count - 1
        head = lax.slice_in_dim(cells, 0, width, axis=dim)
        tail = lax.slice_in_dim(cells, cells.shape[dim] - width, cells.shape[dim], axis=dim)
        cells = jnp.concatenate(
            [
                lax.ppermute(tail, axis, [(i, (i + 1) % count) for i in range(ends)]),
                cells,
                lax.ppermute(head, axis, [((i + 1) % count, i) for i in range(ends)]),
            ],
            axis=dim,
        )
    return cells


def body(
    edge_field,
    conductance,
    send_index,
    panel_source,
    surface_field,
    near_columns,
    near_tiles,
    far_columns,
    far_ranks,
    far_coupling,
    basis_left,
    basis_right,
):
    highest = lax.Precision.HIGHEST
    groups = lax.axis_size("group")
    local = edge_field.shape[0] * edge_field.shape[1] * edge_field.shape[2]
    slots = send_index.shape[2]
    padded = padded_2(edge_field, (("group", 1), ("member", 2)), 1)
    edge_x = padded[0]
    edge_y = padded[1]
    flux = edge_y[1:, :-1] - edge_y[:-1, :-1] - edge_x[:-1, 1:] + edge_x[:-1, :-1]
    part_x = flux[1:, :-1] - flux[1:, 1:]
    part_y = flux[:-1, 1:] - flux[1:, 1:]
    curl_part = jnp.stack([part_x, part_y]) + conductance * edge_field
    flat_edges = edge_field.reshape(-1)
    sent = flat_edges[send_index[0]]
    received = lax.all_to_all(sent, "group", split_axis=0, concat_axis=0, tiled=True)
    trace = received.reshape(-1)[panel_source]
    within = lax.all_gather(surface_field, "member", axis=0, tiled=True)
    vectors = within[near_columns]
    near_part = jnp.einsum("bnij,bnj->bi", near_tiles, vectors, precision=highest)
    coeffs = jnp.einsum("bkr,bk->br", basis_right, surface_field, precision=highest)
    every_coeff = lax.all_gather(coeffs, ("group", "member"), axis=0, tiled=True)
    picked = every_coeff[far_columns]
    rank_total = picked.shape[2]
    keep = jnp.arange(rank_total, dtype=jnp.int32)[None, None, :] < far_ranks[:, :, None]
    picked = jnp.where(keep, picked, jnp.float32(0.0))
    summed = jnp.einsum("bfrs,bfs->br", far_coupling, picked, precision=highest)
    far_part = jnp.einsum("bkr,br->bk", basis_left, summed, precision=highest)
    surface_out = near_part + far_part + 0.5 * trace
    returned = jax.ops.segment_sum(
        surface_field.reshape(-1), panel_source.reshape(-1), num_segments=groups * slots
    )
    arrived = lax.all_to_all(
        returned.reshape(groups, slots), "group", split_axis=0, concat_axis=0, tiled=True
    )
    added = jax.ops.segment_sum(arrived.reshape(-1), send_index[0].reshape(-1), num_segments=local)
    volume_out = curl_part + added.reshape(edge_field.shape)
    return (volume_out, surface_out)


def solution(mesh):
    placed = (
        P(None, "group", "member"),
        P(None, "group", "member"),
        P(("group", "member"), None, None),
        P(("group", "member"), None),
        P(("group", "member"), None),
        P(("group", "member"), None),
        P(("group", "member"), None, None, None),
        P(("group", "member"), None),
        P(("group", "member"), None),
        P(("group", "member"), None, None, None),
        P(("group", "member"), None, None),
        P(("group", "member"), None, None),
    )
    return jax.shard_map(
        body,
        mesh=mesh,
        in_specs=placed,
        out_specs=(P(None, "group", "member"), P(("group", "member"), None)),
        check_vma=False,
    )
```

profile of v0, /device:TPU:1, one launch (start us, length us, event | category | flops | bytes accessed | tf_op | source)
XLA Modules:
  0.0 216.2 jit_solution(3993861724542586363)
XLA Ops:
  0.7 0.8 fusion.10
  1.5 4.5 %collective-permute-start = (f32[2,1,128]{2,1,0:T(1,128)S(1)}, f32[2,1,128]{2,1,0:T(1,128)S(1)}, u32[]{:S(2)}, u32[]{:S(2)}) collective-permute-start(f32[2,1,128]{2,1,0:T(1,128)S(1)} %get-tuple-element.8), channel_id=1, source_target_pairs={{0,8},{8,16},{16,24},{24,32},{32,40},{40,48},{48,56},{56,64},{64,7... | collective-permute-start | bytes 3080 | tf_op jit(solution)/shard_map/ppermute | solution.py:15
  6.0 9.2 %collective-permute-start.1 = (f32[2,1,128]{2,1,0:T(1,128)S(1)}, f32[2,1,128]{2,1,0:T(1,128)S(1)}, u32[]{:S(2)}, u32[]{:S(2)}) collective-permute-start(f32[2,1,128]{2,1,0:T(1,128)S(1)} %get-tuple-element.9), channel_id=1, source_target_pairs={{8,0},{16,8},{24,16},{32,24},{40,32},{48,40},{56,48},{64,56},{72,6... | collective-permute-start | bytes 3080 | tf_op jit(solution)/shard_map/ppermute | solution.py:17
  15.2 4.2 %scatter_custom_fusion = f32[480]{0:T(512)S(1)} fusion(s32[512]{0:T(512)} %bitcast.74, f32[512]{0:T(512)} %bitcast.70, f32[]{:T(128)} %constant.7.clone.1), kind=kCustom, calls=%fused_computation.34 | custom fusion | flops 512 | bytes 2432 | tf_op jit(solution)/shard_map/scatter-add | solution.py:65
  19.4 0.8 all_to_all.12
  20.2 11.9 %all-to-all-start = ((f32[96,1,5]{2,1,0:T(1,128)}), f32[96,1,5]{2,1,0:T(1,128)S(1)}, u32[]{:S(2)}, u32[]{:S(2)}) async-start(f32[96,1,5]{2,1,0:T(1,128)} %bitcast.6), calls=%async_computation | async-start | bytes 98304 | tf_op jit(solution)/shard_map/all_to_all | solution.py:68
  32.1 0.7 fusion.6
  32.8 0.7 compare_select_fusion
  33.8 1.1 fusion.12
  34.9 108.1 %all-gather.1 = f32[768,4,32]{2,1,0:T(4,128)S(1)} all-gather(f32[1,4,32]{2,1,0:T(4,128)S(1)} %bitcast.68), channel_id=1, replica_groups=mesh['group'=96,'member'=8] {'group','member'}, dimensions={0}, use_global_device_ids=true | all-gather | bytes 393728 | tf_op jit(solution)/shard_map/all_gather | solution.py:57
  143.1 15.7 %all-gather = f32[8,4,128]{2,1,0:T(4,128)S(1)} all-gather(f32[1,4,128]{2,1,0:T(4,128)S(1)} %bitcast.72), channel_id=1, replica_groups=mesh['group'=96,'member'=8] {'member'}, dimensions={0}, use_global_device_ids=true | all-gather | bytes 18432 | tf_op jit(solution)/shard_map/all_gather | solution.py:53
  159.7 2.2 %convolution_bitcast_fusion = f32[4,32,1]{1,2,0:T(1,128)S(1)} fusion(f32[4,16,32,1]{2,3,1,0:T(1,128)S(1)} %bitcast.66, f32[4,16,32,32]{3,2,1,0:T(8,128)} %param.21), kind=kOutput, calls=%fused_computation.6 | convolution fusion | flops 786432 | bytes 270848 | tf_op jit(solution)/shard_map/bfrs,bfs->br/dot_general | solution.py:62
  162.6 1.0 fusion.11
  163.8 3.0 %collective-permute-start.2 = (f32[2,34,1]{2,1,0:T(8,128)S(1)}, f32[2,34,1]{2,1,0:T(8,128)S(1)}, u32[]{:S(2)}, u32[]{:S(2)}) collective-permute-start(f32[2,34,1]{2,1,0:T(8,128)S(1)} %get-tuple-element.6), channel_id=1, source_target_pairs={{0,1},{1,2},{2,3},{3,4},{4,5},{5,6},{6,7},{8,9},{9,10},{10,11},{11... | collective-permute-start | bytes 824 | tf_op jit(solution)/shard_map/ppermute | solution.py:15
  166.8 1.3 collective-permute-start.3
  168.3 3.1 %gather_fusion.2 = f32[480]{0:T(512)S(1)} fusion(f32[8192]{0:T(1024)S(1)} %bitcast.61, s32[1024]{0:T(1024)S(1)} %pad_clamp_fusion.1), kind=kCustom, calls=%fused_computation.2 | custom fusion | bytes 5760 | tf_op jit(solution)/shard_map/gather | solution.py:50
  171.4 0.8 all_to_all.14
  172.4 22.5 %all-to-all-start.1 = ((f32[96,1,5]{2,1,0:T(1,128)}), f32[96,1,5]{2,1,0:T(1,128)S(1)}, u32[]{:S(2)}, u32[]{:S(2)}) async-start(f32[96,1,5]{2,1,0:T(1,128)} %bitcast.32), calls=%async_computation.1 | async-start | bytes 98304 | tf_op jit(solution)/shard_map/all_to_all | solution.py:51
  195.5 0.8 reduce.6
  196.5 10.7 %all-to-all-done.1 = f32[96,1,5]{2,1,0:T(1,128)S(1)} async-done(((f32[96,1,5]{2,1,0:T(1,128)}), f32[96,1,5]{2,1,0:T(1,128)S(1)}, u32[]{:S(2)}, u32[]{:S(2)}) %all-to-all-start.1) | async-done | bytes 1952 | tf_op jit(solution)/shard_map/all_to_all | solution.py:51
  207.2 0.8 reduce.7
  208.1 3.3 %scatter_custom_fusion.1 = f32[8192]{0:T(1024)S(1)} fusion(s32[480]{0:T(512)S(1)} %reshape.103, f32[480]{0:T(512)S(1)} %reshape.105, f32[]{:T(128)} %constant.7.clone.1), kind=kCustom, calls=%fused_computation.22 | custom fusion | flops 480 | bytes 32772 | tf_op jit(solution)/shard_map/scatter-add | solution.py:71
  211.5 3.5 %gather_fusion.3 = f32[512]{0:T(512)S(1)} fusion(f32[480]{0:T(512)S(1)} %reshape.60, s32[1024]{0:T(1024)S(1)} %pad_clamp_fusion), kind=kCustom, calls=%fused_computation.3 | custom fusion | bytes 6144 | tf_op jit(solution)/shard_map/gather | solution.py:52
  215.5 0.6 fusion
  (49 shorter events, 4.1 us)
Async XLA Ops:
  0.6 162.0 %copy-start = (f32[4,4,128,128]{3,2,1,0:T(8,128)S(1)}, f32[4,4,128,128]{3,2,1,0:T(8,128)}, u32[]{:S(2)}) copy-start(f32[4,4,128,128]{3,2,1,0:T(8,128)} %param.18) | copy-start | bytes 3145732
  0.6 142.5 %copy-start.5 = (f32[4,128]{1,0:T(4,128)S(1)}, f32[4,128]{1,0:T(4,128)}, u32[]{:S(2)}) copy-start(f32[4,128]{1,0:T(4,128)} %param.16) | copy-start | bytes 6148
  0.7 142.3 %copy-start.7 = (s32[4,16]{1,0:T(4,128)S(1)}, s32[4,16]{1,0:T(4,128)}, u32[]{:S(2)}) copy-start(s32[4,16]{1,0:T(4,128)} %param.19) | copy-start | bytes 772
  0.7 158.2 %copy-start.8 = (s32[4,4]{1,0:T(4,128)S(1)}, s32[4,4]{1,0:T(4,128)}, u32[]{:S(2)}) copy-start(s32[4,4]{1,0:T(4,128)} %param.17) | copy-start | bytes 196
  0.7 158.9 %copy-start.6 = (s32[4,16]{1,0:T(4,128)S(1)}, s32[4,16]{1,0:T(4,128)}, u32[]{:S(2)}) copy-start(s32[4,16]{1,0:T(4,128)} %param.20) | copy-start | bytes 772
  1.5 162.2 %collective-permute-start = (f32[2,1,128]{2,1,0:T(1,128)S(1)}, f32[2,1,128]{2,1,0:T(1,128)S(1)}, u32[]{:S(2)}, u32[]{:S(2)}) collective-permute-start(f32[2,1,128]{2,1,0:T(1,128)S(1)} %get-tuple-element.8), channel_id=1, source_target_pairs={{0,8},{8,16},{16,24},{24,32},{32,40},{40,48},{48,56},{56,64},{64,7... | collective-permute-start | bytes 3080 | tf_op jit(solution)/shard_map/ppermute | solution.py:15
  6.0 157.7 %collective-permute-start.1 = (f32[2,1,128]{2,1,0:T(1,128)S(1)}, f32[2,1,128]{2,1,0:T(1,128)S(1)}, u32[]{:S(2)}, u32[]{:S(2)}) collective-permute-start(f32[2,1,128]{2,1,0:T(1,128)S(1)} %get-tuple-element.9), channel_id=1, source_target_pairs={{8,0},{16,8},{24,16},{32,24},{40,32},{48,40},{56,48},{64,56},{72,6... | collective-permute-start | bytes 3080 | tf_op jit(solution)/shard_map/ppermute | solution.py:17
  20.2 152.2 %all-to-all-start = ((f32[96,1,5]{2,1,0:T(1,128)}), f32[96,1,5]{2,1,0:T(1,128)S(1)}, u32[]{:S(2)}, u32[]{:S(2)}) async-start(f32[96,1,5]{2,1,0:T(1,128)} %bitcast.6), calls=%async_computation | async-start | bytes 98304 | tf_op jit(solution)/shard_map/all_to_all | solution.py:68
  33.8 128.1 %copy-start.2 = (f32[4,128,32]{1,2,0:T(8,128)S(1)}, f32[4,128,32]{1,2,0:T(8,128)}, u32[]{:S(2)}) copy-start(f32[4,128,32]{1,2,0:T(8,128)} %param.22) | copy-start | bytes 196612
  143.0 20.6 %copy-start.4 = (s32[1,96,5]{1,0,2:T(1,128)S(1)}, s32[1,96,5]{1,0,2:T(1,128)}, u32[]{:S(2)}) copy-start(s32[1,96,5]{1,0,2:T(1,128)} %param.14) | copy-start | bytes 5764
  143.0 20.7 %copy-start.1 = (f32[2,32,128]{2,1,0:T(8,128)S(1)}, f32[2,32,128]{2,1,0:T(8,128)}, u32[]{:S(2)}) copy-start(f32[2,32,128]{2,1,0:T(8,128)} %param.12) | copy-start | bytes 98308
  163.8 8.4 %collective-permute-start.2 = (f32[2,34,1]{2,1,0:T(8,128)S(1)}, f32[2,34,1]{2,1,0:T(8,128)S(1)}, u32[]{:S(2)}, u32[]{:S(2)}) collective-permute-start(f32[2,34,1]{2,1,0:T(8,128)S(1)} %get-tuple-element.6), channel_id=1, source_target_pairs={{0,1},{1,2},{2,3},{3,4},{4,5},{5,6},{6,7},{8,9},{9,10},{10,11},{11... | collective-permute-start | bytes 824 | tf_op jit(solution)/shard_map/ppermute | solution.py:15
  166.8 5.4 %collective-permute-start.3 = (f32[2,34,1]{2,1,0:T(8,128)S(1)}, f32[2,34,1]{2,1,0:T(8,128)S(1)}, u32[]{:S(2)}, u32[]{:S(2)}) collective-permute-start(f32[2,34,1]{2,1,0:T(8,128)S(1)} %get-tuple-element.7), channel_id=1, source_target_pairs={{1,0},{2,1},{3,2},{4,3},{5,4},{6,5},{7,6},{9,8},{10,9},{11,10},{12... | collective-permute-start | bytes 824 | tf_op jit(solution)/shard_map/ppermute | solution.py:17
  172.2 43.3 %copy-start.3 = (f32[2,32,128]{2,1,0:T(8,128)S(1)}, f32[2,32,128]{2,1,0:T(8,128)}, u32[]{:S(2)}) copy-start(f32[2,32,128]{2,1,0:T(8,128)} %param.13) | copy-start | bytes 98308
  172.4 34.8 %all-to-all-start.1 = ((f32[96,1,5]{2,1,0:T(1,128)}), f32[96,1,5]{2,1,0:T(1,128)S(1)}, u32[]{:S(2)}, u32[]{:S(2)}) async-start(f32[96,1,5]{2,1,0:T(1,128)} %bitcast.32), calls=%async_computation.1 | async-start | bytes 98304 | tf_op jit(solution)/shard_map/all_to_all | solution.py:51
where the time goes:
time: 217 us; the launch traced here: 216 us
  blocking collectives  124 us (57%)
  starting transfers between devices  52.3 us (24%)
  other arithmetic  12 us (6%)
  local copies, waits for them, and re-layouts  11.9 us (5%)
  waiting for transfers between devices  10.8 us (5%)
  matrix products  4.41 us (2%)
    all_gather x1, blocking collectives, body(): lax.all_gather(coeffs, ('group', 'member'), axis=0, tiled=True)  108 us
    all_to_all x1, starting transfers between devices, body(): lax.all_to_all(sent, 'group', split_axis=0, concat_axis=0, tiled=True)  22.5 us
    all_gather x1, blocking collectives, body(): within = lax.all_gather(surface_field, 'member', axis=0, tiled=True)  15.7 us
    all_to_all x1, starting transfers between devices, body(): lax.all_to_all(returned.reshape(groups, slots), 'group', split_axis=0, co...  11.9 us
    all_to_all x1, waiting for transfers between devices, body(): lax.all_to_all(sent, 'group', split_axis=0, concat_axis=0, tiled=True)  10.7 us
    ppermute x2, starting transfers between devices, padded_2(): lax.ppermute(head, axis, [((i + 1) % count, i) for i in range(ends)])  10.5 us
    ppermute x2, starting transfers between devices, padded_2(): lax.ppermute(tail, axis, [(i, (i + 1) % count) for i in range(ends)])  7.46 us
  transfers between devices with their start and end apart: 6, of which 1 were waited for; matrix products, arithmetic and copies ran while one was open for 8% of the time, Pallas kernels for 0%

commit v1 on v0

v1 whole, which is shorter than its diff:
```python
import functools

import jax
import jax.numpy as jnp
from jax import lax
from jax.experimental import pallas as pl
from jax.experimental.pallas import tpu as pltpu
from jax.sharding import PartitionSpec as P

F32 = jnp.float32
BF16 = jnp.bfloat16
ROWS = 4
EXTRA = 8


def split3(value):
    first = value.astype(BF16)
    rest = value - first.astype(F32)
    second = rest.astype(BF16)
    third = (rest - second.astype(F32)).astype(BF16)
    return first, second, third


def dot_exact(choice, value, dims):
    total = None
    for part in split3(value):
        term = lax.dot_general(choice, part, (dims, ((), ())), preferred_element_type=F32)
        total = term if total is None else total + term
    return total


def lanes(shape):
    return lax.broadcasted_iota(jnp.int32, shape, len(shape) - 1)


def rows(shape):
    return lax.broadcasted_iota(jnp.int32, shape, len(shape) - 2)


def pack_kernel(groups, slots, where_ref, edge_ref, send_ref, source_ref, surface_ref, right_ref, out_ref):
    blocks, width = surface_ref.shape
    rank = right_ref.shape[2]
    height = edge_ref.shape[1]
    group = where_ref[0]
    coeff = jnp.zeros((1, width), F32)
    for b in range(blocks):
        vector = surface_ref[b : b + 1, :]
        part = lax.dot_general(
            jnp.broadcast_to(vector, (8, width)),
            right_ref[b],
            (((1,), (0,)), ((), ())),
            precision=lax.Precision.HIGHEST,
            preferred_element_type=F32,
        )
        wide = jnp.concatenate([part] * (width // rank), axis=1)[0:1, :]
        coeff = jnp.where(lanes((1, width)) // rank == b, wide, coeff)
    out_ref[pl.ds(0, groups, stride=ROWS), :] = jnp.broadcast_to(coeff, (groups, width))
    edge_x = edge_ref[0]
    edge_y = edge_ref[1]
    last_x = edge_x[height - 1 : height, :]
    beyond = jnp.where(lanes((1, width)) == width - 1, 0.0, pltpu.roll(last_x, width - 1, 1))
    down = last_x - beyond - edge_y[height - 1 : height, :]
    up = edge_y[0:1, :]
    index = rows((groups, width))
    out_ref[pl.ds(1, groups, stride=ROWS), :] = jnp.where(index == group + 1, down, up)
    send = send_ref[0]
    flat = edge_ref[...].reshape(2 * height, width)
    lane = lanes((groups, width))
    tail = jnp.where(lane == 2 * slots, last_x[0:1, 0:1], 0.0)
    parts = split3(flat)
    for s in range(slots):
        column = send[:, s : s + 1]
        choice = (lanes((groups, 2 * height)) == column // width).astype(BF16)
        picked = None
        for part in parts:
            term = lax.dot_general(choice, part, (((1,), (0,)), ((), ())), preferred_element_type=F32)
            picked = term if picked is None else picked + term
        value = jnp.sum(jnp.where(lane == column % width, picked, 0.0), axis=1, keepdims=True)
        tail = jnp.where(lane == s, value, tail)
        total = jnp.zeros((groups, width), F32)
        slot = rows((groups, width)) * slots + s
        for b in range(blocks):
            total = total + jnp.where(source_ref[b : b + 1, :] == slot, surface_ref[b : b + 1, :], 0.0)
        tail = jnp.where(lane == slots + s, jnp.sum(total, axis=1, keepdims=True), tail)
    out_ref[pl.ds(2, groups, stride=ROWS), :] = tail
    out_ref[pl.ds(3, groups, stride=ROWS), :] = jnp.zeros((groups, width), F32)


def spread_kernel(groups, members, slots, where_ref, edge_ref, surface_ref, first_ref, out_ref):
    blocks, width = surface_ref.shape
    height = edge_ref.shape[1]
    group = where_ref[0]
    coeffs = first_ref[pl.ds(0, groups, stride=ROWS), :]
    below = first_ref[pl.ds(lax.min(group + 1, groups - 1) * ROWS + 1, 1), :]
    below = jnp.where(group + 1 < groups, below, 0.0)
    above = first_ref[pl.ds(lax.max(group - 1, 0) * ROWS + 2, 1), :]
    corner = jnp.where(group > 0, above[0:1, 2 * slots : 2 * slots + 1], 0.0)
    edge_x = edge_ref[0]
    edge_y = edge_ref[1]
    next_y = jnp.where(rows((height, width)) == height - 1, below, pltpu.roll(edge_y, height - 1, 0))
    flow = next_y - edge_y + edge_x
    last = (lanes((8, width)) == width - 1).astype(BF16)
    first = (lanes((8, width)) == 0).astype(BF16)
    ends = jnp.concatenate(
        [
            dot_exact(last, flow, ((1,), (1,)))[0:1, :],
            dot_exact(first, edge_x, ((1,), (1,)))[0:1, :],
            jnp.broadcast_to(corner, (1, width - 2 * height)),
        ],
        axis=1,
    )
    rim = jnp.concatenate([surface_ref[...], jnp.broadcast_to(ends, (EXTRA - blocks, width))], axis=0)
    for m in range(members):
        out_ref[m, 0:groups, :] = coeffs
        out_ref[m, groups : groups + EXTRA, :] = rim


def finish_kernel(
    groups,
    members,
    slots,
    where_ref,
    near_columns_ref,
    far_columns_ref,
    far_ranks_ref,
    edge_ref,
    conductance_ref,
    send_ref,
    source_ref,
    first_ref,
    second_ref,
    near_ref,
    coupling_ref,
    left_ref,
    volume_ref,
    surface_ref,
):
    blocks, width = source_ref.shape
    height = edge_ref.shape[1]
    rank = left_ref.shape[2]
    per_member = groups + EXTRA
    group = where_ref[0]
    member = where_ref[1]
    highest = lax.Precision.HIGHEST

    tail = first_ref[pl.ds(2, groups, stride=ROWS), :]
    ones_near = jnp.ones((8, width), F32)
    ones_far = jnp.ones((8, rank), F32)
    for b in range(blocks):
        total = jnp.zeros((width, width), F32)
        for n in range(near_ref.shape[1]):
            column = near_columns_ref[b, n]
            row = (column // blocks) * per_member + groups + column % blocks
            total = total + near_ref[b, n] * second_ref[pl.ds(row, 1), :]
        near = lax.dot_general(
            ones_near, total, (((1,), (1,)), ((), ())), precision=highest, preferred_element_type=F32
        )
        total = jnp.zeros((rank, rank), F32)
        for f in range(coupling_ref.shape[1]):
            column = far_columns_ref[b, f]
            device = column // blocks
            row = (device % members) * per_member + device // members
            picked = second_ref[pl.ds(row, 1), :]
            shift = (width - (column % blocks) * rank) % width
            picked = pltpu.roll(jnp.broadcast_to(picked, (8, width)), shift, 1)[0:1, :]
            picked = jnp.where(lanes((1, width)) < far_ranks_ref[b, f], picked, 0.0)
            total = total + coupling_ref[b, f] * picked[:, 0:rank]
        summed = lax.dot_general(
            ones_far, total, (((1,), (1,)), ((), ())), precision=highest, preferred_element_type=F32
        )
        far = lax.dot_general(
            summed, left_ref[b], (((1,), (1,)), ((), ())), precision=highest, preferred_element_type=F32
        )
        trace = jnp.zeros((groups, width), F32)
        for s in range(slots):
            slot = rows((groups, width)) * slots + s
            trace = trace + jnp.where(source_ref[b : b + 1, :] == slot, tail[:, s : s + 1], 0.0)
        trace = jnp.sum(trace, axis=0, keepdims=True)
        surface_ref[b : b + 1, :] = near[0:1, :] + far[0:1, :] + 0.5 * trace

    send = send_ref[0]
    added = None
    for s in range(slots):
        column = send[:, s : s + 1]
        choice = (lanes((groups, 2 * height)) == column // width).astype(BF16)
        value = jnp.where(lanes((groups, width)) == column % width, tail[:, slots + s : slots + s + 1], 0.0)
        term = dot_exact(choice, value, ((0,), (0,)))
        added = term if added is None else added + term

    edge_x = edge_ref[0]
    edge_y = edge_ref[1]
    shape = (height, width)
    lane = lanes(shape)
    line = rows(shape)
    below = first_ref[pl.ds(lax.min(group + 1, groups - 1) * ROWS + 1, 1), :]
    below = jnp.where(group + 1 < groups, below, 0.0)
    above = first_ref[pl.ds(lax.max(group - 1, 0) * ROWS + 1, 1), :]
    above = jnp.where(group > 0, above, 0.0)
    before = second_ref[pl.ds(lax.max(member - 1, 0) * per_member + groups + blocks, 1), :]
    before = jnp.where(member > 0, before, 0.0)
    after = second_ref[pl.ds(lax.min(member + 1, members - 1) * per_member + groups + blocks, 1), :]
    after = jnp.where(member + 1 < members, after, 0.0)

    def upright(row, start):
        wide = jnp.where(lanes((height, width)) == rows((height, width)) + start, row, 0.0)
        return jnp.sum(wide, axis=1, keepdims=True)

    next_x = jnp.where(lane == width - 1, upright(after, height), pltpu.roll(edge_x, width - 1, 1))
    next_y = jnp.where(line == height - 1, below, pltpu.roll(edge_y, height - 1, 0))
    flux = next_y - edge_y - next_x + edge_x
    left = upright(before, 0) - edge_x[:, 0:1]
    flux_left = jnp.where(lane == 0, left, pltpu.roll(flux, 1, 1))
    corner = after[0:1, 2 * height : 2 * height + 1]
    top = edge_y[0:1, :] + above - jnp.where(lanes((1, width)) == width - 1, corner, 0.0)
    flux_up = jnp.where(line == 0, top, pltpu.roll(flux, 1, 0))
    volume_ref[0] = flux_left - flux + conductance_ref[0] * edge_x + added[0:height, :]
    volume_ref[1] = flux_up - flux + conductance_ref[1] * edge_y + added[height : 2 * height, :]


def vmem(count):
    return [pl.BlockSpec(memory_space=pltpu.VMEM)] * count


def smem(count):
    return [pl.BlockSpec(memory_space=pltpu.SMEM)] * count


PARAMS = pltpu.CompilerParams(vmem_limit_bytes=16 * 1024 * 1024)


def body(
    edge_field,
    conductance,
    send_index,
    panel_source,
    surface_field,
    near_columns,
    near_tiles,
    far_columns,
    far_ranks,
    far_coupling,
    basis_left,
    basis_right,
):
    groups = lax.axis_size("group")
    members = lax.axis_size("member")
    slots = send_index.shape[2]
    blocks, width = surface_field.shape
    where = jnp.stack([lax.axis_index("group"), lax.axis_index("member")]).astype(jnp.int32)
    with jax.named_scope("pack"):
        first = pl.pallas_call(
            functools.partial(pack_kernel, groups, slots),
            out_shape=jax.ShapeDtypeStruct((groups * ROWS, width), F32),
            in_specs=smem(1) + vmem(5),
            out_specs=pl.BlockSpec(memory_space=pltpu.VMEM),
            compiler_params=PARAMS,
        )(where, edge_field, send_index, panel_source, surface_field, basis_right)
    first = lax.all_to_all(
        first.reshape(groups, ROWS, width), "group", split_axis=0, concat_axis=0, tiled=True
    ).reshape(groups * ROWS, width)
    with jax.named_scope("spread"):
        second = pl.pallas_call(
            functools.partial(spread_kernel, groups, members, slots),
            out_shape=jax.ShapeDtypeStruct((members, groups + EXTRA, width), F32),
            in_specs=smem(1) + vmem(3),
            out_specs=pl.BlockSpec(memory_space=pltpu.VMEM),
            compiler_params=PARAMS,
        )(where, edge_field, surface_field, first)
    second = lax.all_to_all(second, "member", split_axis=0, concat_axis=0, tiled=True)
    second = second.reshape(members * (groups + EXTRA), width)
    with jax.named_scope("finish"):
        return pl.pallas_call(
            functools.partial(finish_kernel, groups, members, slots),
            out_shape=(
                jax.ShapeDtypeStruct(edge_field.shape, F32),
                jax.ShapeDtypeStruct(surface_field.shape, F32),
            ),
            in_specs=smem(4) + vmem(9),
            out_specs=tuple(vmem(2)),
            compiler_params=PARAMS,
        )(
            where,
            near_columns,
            far_columns,
            far_ranks,
            edge_field,
            conductance,
            send_index,
            panel_source,
            first,
            second,
            near_tiles,
            far_coupling,
            basis_left,
        )


def solution(mesh):
    both = ("group", "member")
    placed = (
        P(None, "group", "member"),
        P(None, "group", "member"),
        P(both, None, None),
        P(both, None),
        P(both, None),
        P(both, None),
        P(both, None, None, None),
        P(both, None),
        P(both, None),
        P(both, None, None, None),
        P(both, None, None),
        P(both, None, None),
    )
    return jax.shard_map(
        body,
        mesh=mesh,
        in_specs=placed,
        out_specs=(P(None, "group", "member"), P(both, None)),
        check_vma=False,
    )
```

time: 217 us -> 69.1 us (0.32)
  blocking collectives: 124 us -> 36.5 us
  starting transfers between devices: 52.3 us -> 6.82 us
  other arithmetic: 12 us -> 0.08 us
  local copies, waits for them, and re-layouts: 11.9 us -> 2.53 us
  Pallas kernels: 0 us -> 6.46 us
  waiting for transfers between devices: 10.8 us -> 15.7 us
  matrix products: 4.41 us -> 0 us
    all_gather x2 -> x0, blocking collectives: 124 us -> none  [the longest x1 108 us: body(): lax.all_gather(coeffs, ('group', 'member'), axis=0, tiled=True)]
    all_to_all x0 -> x1, blocking collectives: none -> 36.5 us  [body(): lax.all_to_all(first.reshape(groups, ROWS, width), 'group', split_axis=0,...]
    all_to_all x2 -> x1, starting transfers between devices: 34.4 us -> 6.82 us  [body(): lax.all_to_all(second, 'member', split_axis=0, concat_axis=0, tiled=True)]
    ppermute x4 -> x0, starting transfers between devices: 18 us -> none  [the longest x2 10.5 us: padded_2(): lax.ppermute(head, axis, [((i + 1) % count, i) for i in range(ends)])]
    gather x4 -> x0, local copies, waits for them, and re-layouts: 7.8 us -> none  [the longest x1 3.49 us: body(): trace = received.reshape(-1)[panel_source]]
    scatter-add x2 -> x0, other arithmetic: 7.53 us -> none  [the longest x1 4.23 us: body(): jax.ops.segment_sum(surface_field.reshape(-1), panel_source.reshape(-1),...]
    pallas_call x0 -> x3, Pallas kernels: none -> 6.46 us  [the longest x1 3.75 us: body(): pl.pallas_call(functools.partial(finish_kernel, groups, members, slots),...]
    all_to_all x2 -> x1, waiting for transfers between devices: 10.7 us -> 15.7 us  [body(): lax.all_to_all(second, 'member', split_axis=0, concat_axis=0, tiled=True)]
  transfers between devices with their start and end apart: 6 -> 1, of which waited for: 1 -> 1; matrix products, arithmetic and copies ran while one was open for 8% -> 0% of each run, Pallas kernels for 0% -> 0%
where the time goes in v1:
time: 69.1 us; the launch traced here: 68.8 us
  blocking collectives  36.5 us (53%)
  waiting for transfers between devices  15.7 us (23%)
  starting transfers between devices  6.82 us (10%)
  Pallas kernels  6.46 us (9%)
  local copies, waits for them, and re-layouts  2.53 us (4%)
  between operations  0.77 us (1%)
    all_to_all x1, blocking collectives, body(): lax.all_to_all(first.reshape(groups, ROWS, width), 'group', split_axis=0,...  36.5 us
    all_to_all x1, waiting for transfers between devices, body(): lax.all_to_all(second, 'member', split_axis=0, concat_axis=0, tiled=True)  15.7 us
    all_to_all x1, starting transfers between devices, body(): lax.all_to_all(second, 'member', split_axis=0, concat_axis=0, tiled=True)  6.82 us
    pallas_call x1, Pallas kernels, body(): pl.pallas_call(functools.partial(finish_kernel, groups, members, slots),...  3.75 us
    unnamed x25, local copies, waits for them, and re-layouts  2.53 us
    pallas_call x1, Pallas kernels, body(): pl.pallas_call(functools.partial(spread_kernel, groups, members, slots),...  1.51 us
  transfers between devices with their start and end apart: 1, of which 1 were waited for; matrix products, arithmetic and copies ran while one was open for 0% of the time, Pallas kernels for 0%

profile of v1, /device:TPU:1, one launch (start us, length us, event | category | flops | bytes accessed | tf_op | source)
XLA Modules:
  0.0 68.8 jit_solution(5733782603762503752)
XLA Ops:
  0.6 0.0 copy-start.10
  0.6 0.7 copy-done.10
  1.3 0.1 copy.16.send_ref
  1.4 1.0 %copy.15.right_ref = f32[4,128,32]{2,1,0:T(8,128)S(1)} copy(f32[4,128,32]{1,2,0:T(8,128)} %param.23) | data formatting | bytes 131072 | tf_op args[11]
  2.4 0.0 copy-start.5
  2.4 0.0 copy-start.4
  2.4 0.1 pad_add_fusion.where_ref
  2.5 0.6 copy-done.5
  3.1 0.0 copy-done.4
  3.1 1.2 %pack.1 = f32[384,128]{1,0:T(8,128)S(1)} custom-call(s32[2]{0:T(128)S(1)} %pad_add_fusion.where_ref, f32[2,32,128]{2,1,0:T(8,128)S(1)} %copy-done.2, s32[1,96,5]{2,1,0:T(8,128)S(1)} %copy.16.send_ref, s32[4,128]{1,0:T(4,128)S(1)} %copy-done.5, f32[4,128]{1,0:T(4,128)S(1)} %copy-done.4, f32[4,128,32]{2,1,0:T(8,128)S(1)} %copy.15.right_ref), custom_call_target="tpu_custom_call" | custom-call | tf_op jit(solution)/shard_map/pack/pallas_call | solution.py:251
  4.3 0.0 copy-start
  4.3 0.0 copy-start.1
  4.3 36.5 %all_to_all.10 = f32[96,4,128]{2,1,0:T(4,128)S(1)} all-to-all(f32[96,4,128]{2,1,0:T(4,128)S(1)} %bitcast.8), channel_id=1, replica_groups=mesh['group'=96,'member'=8] {'group'}, dimensions={0} | all-to-all | bytes 393216 | tf_op jit(solution)/shard_map/all_to_all | solution.py:258
  40.8 1.5 %spread.1 = f32[8,104,128]{2,1,0:T(8,128)} custom-call(s32[2]{0:T(128)S(1)} %pad_add_fusion.where_ref, f32[2,32,128]{2,1,0:T(8,128)S(1)} %copy-done.2, f32[4,128]{1,0:T(4,128)S(1)} %copy-done.4, f32[384,128]{1,0:T(8,128)S(1)} %bitcast.5), custom_call_target="tpu_custom_call" | custom-call | tf_op jit(solution)/shard_map/spread/pallas_call | solution.py:262
  42.3 6.8 %all-to-all-start.1 = ((f32[8,104,128]{2,1,0:T(8,128)}), f32[8,104,128]{2,1,0:T(8,128)S(1)}, u32[]{:S(2)}, u32[]{:S(2)}) async-start(f32[8,104,128]{2,1,0:T(8,128)} %spread.1), calls=%async_computation.1 | async-start | bytes 851968 | tf_op jit(solution)/shard_map/all_to_all | solution.py:269
  49.2 0.0 copy-start.3
  49.2 0.0 copy-start.6
  49.2 0.0 copy-start.7
  49.2 0.0 copy-start.8
  49.2 0.1 copy.17.left_ref
  49.4 15.7 %all-to-all-done.1 = f32[8,104,128]{2,1,0:T(8,128)S(1)} async-done(((f32[8,104,128]{2,1,0:T(8,128)}), f32[8,104,128]{2,1,0:T(8,128)S(1)}, u32[]{:S(2)}, u32[]{:S(2)}) %all-to-all-start.1) | async-done | bytes 426016 | tf_op jit(solution)/shard_map/all_to_all | solution.py:269
  65.0 0.0 copy-done.6
  65.0 0.0 copy-done.7
  65.1 3.8 %finish.1 = (f32[2,32,128]{2,1,0:T(8,128)}, f32[4,128]{1,0:T(4,128)}) custom-call(s32[2]{0:T(128)S(1)} %pad_add_fusion.where_ref, s32[4,4]{1,0:T(4,128)S(1)} %copy-done.6, s32[4,16]{1,0:T(4,128)S(1)} %copy-done.7, s32[4,16]{1,0:T(4,128)S(1)} %copy-done.8, f32[2,32,128]{2,1,0:T(8,128)S(1)} %copy-done.2, f32[2,32,128]{2,1,0:T(8,128)S(1)} %copy-done.3, ...), custom_call_target="tpu_custom_call" | custom-call | tf_op jit(solution)/shard_map/finish/pallas_call | solution.py:272
  (8 shorter events, 0.0 us)
Async XLA Ops:
  0.6 0.7 copy-start.10
  1.4 1.1 %copy-start.2 = (f32[2,32,128]{2,1,0:T(8,128)S(1)}, f32[2,32,128]{2,1,0:T(8,128)}, u32[]{:S(2)}) copy-start(f32[2,32,128]{2,1,0:T(8,128)} %edge_ref.5) | copy-start | bytes 98308
  2.4 0.7 copy-start.5
  2.4 0.7 %copy-start.4 = (f32[4,128]{1,0:T(4,128)S(1)}, f32[4,128]{1,0:T(4,128)}, u32[]{:S(2)}) copy-start(f32[4,128]{1,0:T(4,128)} %surface_ref.3) | copy-start | bytes 6148
  3.1 46.0 %copy-start.9 = (f32[4,128,32]{1,2,0:T(8,128)S(1)}, f32[4,128,32]{1,2,0:T(8,128)}, u32[]{:S(2)}) copy-start(f32[4,128,32]{1,2,0:T(8,128)} %param.22) | copy-start | bytes 196612
  4.3 60.7 %copy-start = (f32[4,4,128,128]{3,2,1,0:T(8,128)S(1)}, f32[4,4,128,128]{3,2,1,0:T(8,128)}, u32[]{:S(2)}) copy-start(f32[4,4,128,128]{3,2,1,0:T(8,128)} %near_ref.1) | copy-start | bytes 3145732
  4.3 60.7 %copy-start.1 = (f32[4,16,32,32]{3,2,1,0:T(8,128)S(1)}, f32[4,16,32,32]{3,2,1,0:T(8,128)}, u32[]{:S(2)}) copy-start(f32[4,16,32,32]{3,2,1,0:T(8,128)} %coupling_ref.1) | copy-start | bytes 786436
  42.3 22.7 %all-to-all-start.1 = ((f32[8,104,128]{2,1,0:T(8,128)}), f32[8,104,128]{2,1,0:T(8,128)S(1)}, u32[]{:S(2)}, u32[]{:S(2)}) async-start(f32[8,104,128]{2,1,0:T(8,128)} %spread.1), calls=%async_computation.1 | async-start | bytes 851968 | tf_op jit(solution)/shard_map/all_to_all | solution.py:269
  49.2 15.9 %copy-start.3 = (f32[2,32,128]{2,1,0:T(8,128)S(1)}, f32[2,32,128]{2,1,0:T(8,128)}, u32[]{:S(2)}) copy-start(f32[2,32,128]{2,1,0:T(8,128)} %conductance_ref.1) | copy-start | bytes 98308
  49.2 15.8 %copy-start.6 = (s32[4,4]{1,0:T(4,128)S(1)}, s32[4,4]{1,0:T(4,128)}, u32[]{:S(2)}) copy-start(s32[4,4]{1,0:T(4,128)} %near_columns_ref.1) | copy-start | bytes 196
  49.2 15.8 %copy-start.7 = (s32[4,16]{1,0:T(4,128)S(1)}, s32[4,16]{1,0:T(4,128)}, u32[]{:S(2)}) copy-start(s32[4,16]{1,0:T(4,128)} %far_columns_ref.1) | copy-start | bytes 772
  49.2 15.8 %copy-start.8 = (s32[4,16]{1,0:T(4,128)S(1)}, s32[4,16]{1,0:T(4,128)}, u32[]{:S(2)}) copy-start(s32[4,16]{1,0:T(4,128)} %far_ranks_ref.1) | copy-start | bytes 772

commit v2 on v1

--- a/solution.py
+++ b/solution.py
@@ -39,21 +39,18 @@
 
 def pack_kernel(groups, slots, where_ref, edge_ref, send_ref, source_ref, surface_ref, right_ref, out_ref):
     blocks, width = surface_ref.shape
-    rank = right_ref.shape[2]
+    rank = right_ref.shape[1]
     height = edge_ref.shape[1]
     group = where_ref[0]
-    coeff = jnp.zeros((1, width), F32)
-    for b in range(blocks):
-        vector = surface_ref[b : b + 1, :]
-        part = lax.dot_general(
-            jnp.broadcast_to(vector, (8, width)),
-            right_ref[b],
-            (((1,), (0,)), ((), ())),
-            precision=lax.Precision.HIGHEST,
-            preferred_element_type=F32,
-        )
-        wide = jnp.concatenate([part] * (width // rank), axis=1)[0:1, :]
-        coeff = jnp.where(lanes((1, width)) // rank == b, wide, coeff)
+    every = lax.dot_general(
+        surface_ref[...],
+        right_ref[...].reshape(blocks * rank, width),
+        (((1,), (1,)), ((), ())),
+        precision=lax.Precision.HIGHEST,
+        preferred_element_type=F32,
+    )
+    own = lanes((blocks, blocks * rank)) // rank == rows((blocks, blocks * rank))
+    coeff = jnp.sum(jnp.where(own, every, 0.0), axis=0, keepdims=True)
     out_ref[pl.ds(0, groups, stride=ROWS), :] = jnp.broadcast_to(coeff, (groups, width))
     edge_x = edge_ref[0]
     edge_y = edge_ref[1]
@@ -137,24 +134,22 @@
 ):
     blocks, width = source_ref.shape
     height = edge_ref.shape[1]
-    rank = left_ref.shape[2]
+    rank = left_ref.shape[1]
     per_member = groups + EXTRA
     group = where_ref[0]
     member = where_ref[1]
     highest = lax.Precision.HIGHEST
 
     tail = first_ref[pl.ds(2, groups, stride=ROWS), :]
-    ones_near = jnp.ones((8, width), F32)
-    ones_far = jnp.ones((8, rank), F32)
+    sums = []
+    fars = []
     for b in range(blocks):
         total = jnp.zeros((width, width), F32)
         for n in range(near_ref.shape[1]):
             column = near_columns_ref[b, n]
             row = (column // blocks) * per_member + groups + column % blocks
             total = total + near_ref[b, n] * second_ref[pl.ds(row, 1), :]
-        near = lax.dot_general(
-            ones_near, total, (((1,), (1,)), ((), ())), precision=highest, preferred_element_type=F32
-        )
+        sums.append(total)
         total = jnp.zeros((rank, rank), F32)
         for f in range(coupling_ref.shape[1]):
             column = far_columns_ref[b, f]
@@ -165,18 +160,36 @@
             picked = pltpu.roll(jnp.broadcast_to(picked, (8, width)), shift, 1)[0:1, :]
             picked = jnp.where(lanes((1, width)) < far_ranks_ref[b, f], picked, 0.0)
             total = total + coupling_ref[b, f] * picked[:, 0:rank]
-        summed = lax.dot_general(
-            ones_far, total, (((1,), (1,)), ((), ())), precision=highest, preferred_element_type=F32
-        )
-        far = lax.dot_general(
-            summed, left_ref[b], (((1,), (1,)), ((), ())), precision=highest, preferred_element_type=F32
-        )
+        fars.append(total)
+    near = lax.dot_general(
+        jnp.ones((8, width), F32),
+        jnp.concatenate(sums, axis=0),
+        (((1,), (1,)), ((), ())),
+        precision=highest,
+        preferred_element_type=F32,
+    )
+    summed = lax.dot_general(
+        jnp.ones((8, rank), F32),
+        jnp.concatenate(fars, axis=0),
+        (((1,), (1,)), ((), ())),
+        precision=highest,
+        preferred_element_type=F32,
+    )
+    own = lanes(summed.shape) // rank == rows(summed.shape)
+    far = lax.dot_general(
+        jnp.where(own, summed, 0.0),
+        left_ref[...].reshape(blocks * rank, width),
+        (((1,), (0,)), ((), ())),
+        precision=highest,
+        preferred_element_type=F32,
+    )
+    for b in range(blocks):
         trace = jnp.zeros((groups, width), F32)
         for s in range(slots):
             slot = rows((groups, width)) * slots + s
             trace = trace + jnp.where(source_ref[b : b + 1, :] == slot, tail[:, s : s + 1], 0.0)
         trace = jnp.sum(trace, axis=0, keepdims=True)
-        surface_ref[b : b + 1, :] = near[0:1, :] + far[0:1, :] + 0.5 * trace
+        surface_ref[b : b + 1, :] = near[0:1, b * width : (b + 1) * width] + far[b : b + 1, :] + 0.5 * trace
 
     send = send_ref[0]
     added = None
@@ -254,7 +267,7 @@
             in_specs=smem(1) + vmem(5),
             out_specs=pl.BlockSpec(memory_space=pltpu.VMEM),
             compiler_params=PARAMS,
-        )(where, edge_field, send_index, panel_source, surface_field, basis_right)
+        )(where, edge_field, send_index, panel_source, surface_field, jnp.swapaxes(basis_right, 1, 2))
     first = lax.all_to_all(
         first.reshape(groups, ROWS, width), "group", split_axis=0, concat_axis=0, tiled=True
     ).reshape(groups * ROWS, width)
@@ -291,7 +304,7 @@
             second,
             near_tiles,
             far_coupling,
-            basis_left,
+            jnp.swapaxes(basis_left, 1, 2),
         )
 
 

time: 69.1 us -> 67 us (0.970)
  blocking collectives: 36.5 us -> 57.8 us
  waiting for transfers between devices: 15.7 us -> 0 us
  starting transfers between devices: 6.82 us -> 0 us
  Pallas kernels: 6.46 us -> 5.13 us
    all_to_all x0 -> x1, blocking collectives: none -> 21.5 us  [body(): lax.all_to_all(second, 'member', split_axis=0, concat_axis=0, tiled=True)]
    all_to_all x1 -> x0, waiting for transfers between devices: 15.7 us -> none  [body(): lax.all_to_all(second, 'member', split_axis=0, concat_axis=0, tiled=True)]
    all_to_all x1 -> x0, starting transfers between devices: 6.82 us -> none  [body(): lax.all_to_all(second, 'member', split_axis=0, concat_axis=0, tiled=True)]
    pallas_call x1, Pallas kernels: 1.51 us -> 0.76 us  [body(): pl.pallas_call(functools.partial(spread_kernel, groups, members, slots),...]
  transfers between devices with their start and end apart: 1 -> 0, of which waited for: 1 -> 0; matrix products, arithmetic and copies ran while one was open for 0% -> 0% of each run, Pallas kernels for 0% -> 0%
where the time goes in v2:
time: 67 us; the launch traced here: 66.6 us
  blocking collectives  57.8 us (86%)
  Pallas kernels  5.13 us (8%)
  local copies, waits for them, and re-layouts  2.88 us (4%)
  between operations  0.74 us (1%)
    all_to_all x1, blocking collectives, body(): lax.all_to_all(first.reshape(groups, ROWS, width), 'group', split_axis=0,...  36.3 us
    all_to_all x1, blocking collectives, body(): lax.all_to_all(second, 'member', split_axis=0, concat_axis=0, tiled=True)  21.5 us
    pallas_call x1, Pallas kernels, body(): pl.pallas_call(functools.partial(finish_kernel, groups, members, slots),...  3.25 us
    unnamed x25, local copies, waits for them, and re-layouts  2.88 us

profile of v2, /device:TPU:1, one launch (start us, length us, event | category | flops | bytes accessed | tf_op | source)
XLA Modules:
  0.0 66.6 jit_solution(5948194245602918160)
XLA Ops:
  0.6 0.0 copy-start.11
  0.6 0.0 copy-start.2
  0.7 0.7 copy-done.11
  1.3 0.1 copy.15.send_ref
  1.4 0.0 copy-start.6
  1.4 0.1 pad_add_fusion.where_ref
  1.5 0.0 copy-done.2
  1.5 0.6 copy-done.7
  2.1 0.0 copy-done.6
  2.1 0.8 %copy-done.4 = f32[4,128,32]{1,2,0:T(8,128)S(1)} copy-done((f32[4,128,32]{1,2,0:T(8,128)S(1)}, f32[4,128,32]{1,2,0:T(8,128)}, u32[]{:S(2)}) %copy-start.4) | copy-done | bytes 65560
  3.0 1.1 %pack.1 = f32[384,128]{1,0:T(8,128)S(1)} custom-call(s32[2]{0:T(128)S(1)} %pad_add_fusion.where_ref, f32[2,32,128]{2,1,0:T(8,128)S(1)} %copy-done.2, s32[1,96,5]{2,1,0:T(8,128)S(1)} %copy.15.send_ref, s32[4,128]{1,0:T(4,128)S(1)} %copy-done.7, f32[4,128]{1,0:T(4,128)S(1)} %copy-done.6, f32[4,32,128]{2,1,0:T(8,128)S(1)} %bitcast.12), custom_call_target="tpu_custom_call" | custom-call | tf_op jit(solution)/shard_map/pack/pallas_call | solution.py:264
  4.1 36.3 %all_to_all.10 = f32[96,4,128]{2,1,0:T(4,128)S(1)} all-to-all(f32[96,4,128]{2,1,0:T(4,128)S(1)} %bitcast.10), channel_id=1, replica_groups=mesh['group'=96,'member'=8] {'group'}, dimensions={0} | all-to-all | bytes 393216 | tf_op jit(solution)/shard_map/all_to_all | solution.py:271
  40.4 0.8 %spread.1 = f32[8,104,128]{2,1,0:T(8,128)S(1)} custom-call(s32[2]{0:T(128)S(1)} %pad_add_fusion.where_ref, f32[2,32,128]{2,1,0:T(8,128)S(1)} %copy-done.2, f32[4,128]{1,0:T(4,128)S(1)} %copy-done.6, f32[384,128]{1,0:T(8,128)S(1)} %bitcast.7), custom_call_target="tpu_custom_call" | custom-call | tf_op jit(solution)/shard_map/spread/pallas_call | solution.py:275
  41.2 0.0 copy-start.5
  41.2 0.0 copy-start.9
  41.2 0.0 copy-start.10
  41.2 21.5 %all_to_all.11 = f32[8,104,128]{2,1,0:T(8,128)S(1)} all-to-all(f32[8,104,128]{2,1,0:T(8,128)S(1)} %spread.1), channel_id=1, replica_groups=mesh['group'=96,'member'=8] {'member'}, dimensions={0} | all-to-all | bytes 851968 | tf_op jit(solution)/shard_map/all_to_all | solution.py:282
  62.7 0.0 copy-done
  62.7 0.0 copy-done.1
  62.7 0.0 copy-done.3
  62.7 0.0 copy-done.5
  62.7 0.0 copy-done.9
  62.8 0.6 copy-done.8
  63.4 3.2 %finish.1 = (f32[2,32,128]{2,1,0:T(8,128)}, f32[4,128]{1,0:T(4,128)}) custom-call(s32[2]{0:T(128)S(1)} %pad_add_fusion.where_ref, s32[4,4]{1,0:T(4,128)S(1)} %copy-done.8, s32[4,16]{1,0:T(4,128)S(1)} %copy-done.9, s32[4,16]{1,0:T(4,128)S(1)} %copy-done.10, f32[2,32,128]{2,1,0:T(8,128)S(1)} %copy-done.2, f32[2,32,128]{2,1,0:T(8,128)S(1)} %copy-done.5, ...), custom_call_target="tpu_custom_call" | custom-call | tf_op jit(solution)/shard_map/finish/pallas_call | solution.py:285
  (7 shorter events, 0.0 us)
Async XLA Ops:
  0.6 0.7 %copy-start.11 = (s32[1,96,5]{1,0,2:T(1,128)S(1)}, s32[1,96,5]{1,0,2:T(1,128)}, u32[]{:S(2)}) copy-start(s32[1,96,5]{1,0,2:T(1,128)} %param.14) | copy-start | bytes 5764
  0.6 0.9 %copy-start.2 = (f32[2,32,128]{2,1,0:T(8,128)S(1)}, f32[2,32,128]{2,1,0:T(8,128)}, u32[]{:S(2)}) copy-start(f32[2,32,128]{2,1,0:T(8,128)} %edge_ref.5) | copy-start | bytes 98308
  1.4 0.7 %copy-start.7 = (s32[4,128]{1,0:T(4,128)S(1)}, s32[4,128]{1,0:T(4,128)}, u32[]{:S(2)}) copy-start(s32[4,128]{1,0:T(4,128)} %source_ref.3) | copy-start | bytes 6148
  1.4 0.7 %copy-start.6 = (f32[4,128]{1,0:T(4,128)S(1)}, f32[4,128]{1,0:T(4,128)}, u32[]{:S(2)}) copy-start(f32[4,128]{1,0:T(4,128)} %surface_ref.3) | copy-start | bytes 6148
  2.1 0.8 %copy-start.4 = (f32[4,128,32]{1,2,0:T(8,128)S(1)}, f32[4,128,32]{1,2,0:T(8,128)}, u32[]{:S(2)}) copy-start(f32[4,128,32]{1,2,0:T(8,128)} %param.23) | copy-start | bytes 196612
  3.0 59.8 %copy-start = (f32[4,4,128,128]{3,2,1,0:T(8,128)S(1)}, f32[4,4,128,128]{3,2,1,0:T(8,128)}, u32[]{:S(2)}) copy-start(f32[4,4,128,128]{3,2,1,0:T(8,128)} %near_ref.1) | copy-start | bytes 3145732
  3.0 59.8 %copy-start.1 = (f32[4,16,32,32]{3,2,1,0:T(8,128)S(1)}, f32[4,16,32,32]{3,2,1,0:T(8,128)}, u32[]{:S(2)}) copy-start(f32[4,16,32,32]{3,2,1,0:T(8,128)} %coupling_ref.1) | copy-start | bytes 786436
  41.2 21.5 %copy-start.3 = (f32[4,128,32]{1,2,0:T(8,128)S(1)}, f32[4,128,32]{1,2,0:T(8,128)}, u32[]{:S(2)}) copy-start(f32[4,128,32]{1,2,0:T(8,128)} %param.22) | copy-start | bytes 196612
  41.2 21.5 %copy-start.5 = (f32[2,32,128]{2,1,0:T(8,128)S(1)}, f32[2,32,128]{2,1,0:T(8,128)}, u32[]{:S(2)}) copy-start(f32[2,32,128]{2,1,0:T(8,128)} %conductance_ref.1) | copy-start | bytes 98308
  41.2 21.5 %copy-start.9 = (s32[4,16]{1,0:T(4,128)S(1)}, s32[4,16]{1,0:T(4,128)}, u32[]{:S(2)}) copy-start(s32[4,16]{1,0:T(4,128)} %far_columns_ref.1) | copy-start | bytes 772
  41.2 21.5 %copy-start.10 = (s32[4,16]{1,0:T(4,128)S(1)}, s32[4,16]{1,0:T(4,128)}, u32[]{:S(2)}) copy-start(s32[4,16]{1,0:T(4,128)} %far_ranks_ref.1) | copy-start | bytes 772
  62.7 0.7 %copy-start.8 = (s32[4,4]{1,0:T(4,128)S(1)}, s32[4,4]{1,0:T(4,128)}, u32[]{:S(2)}) copy-start(s32[4,4]{1,0:T(4,128)} %near_columns_ref.1) | copy-start | bytes 196

commit v3 on v0

v3 whole, which is shorter than its diff:
```python
import functools

import jax
import jax.numpy as jnp
from jax import lax
from jax.experimental import pallas as pl
from jax.experimental.pallas import tpu as pltpu
from jax.sharding import PartitionSpec as P

F32 = jnp.float32
BF16 = jnp.bfloat16
HIGHEST = lax.Precision.HIGHEST
CORES = 2
ROWS = 3
EXTRA = 8
SIDE = 8


def split3(value):
    first = value.astype(BF16)
    rest = value - first.astype(F32)
    second = rest.astype(BF16)
    third = (rest - second.astype(F32)).astype(BF16)
    return first, second, third


def dot_exact(choice, value, dims):
    total = None
    for part in split3(value):
        term = lax.dot_general(choice, part, (dims, ((), ())), preferred_element_type=F32)
        total = term if total is None else total + term
    return total


def dot_full(left, right, dims):
    return lax.dot_general(left, right, (dims, ((), ())), precision=HIGHEST, preferred_element_type=F32)


def lanes(shape):
    return lax.broadcasted_iota(jnp.int32, shape, len(shape) - 1)


def rows(shape):
    return lax.broadcasted_iota(jnp.int32, shape, len(shape) - 2)


def upright(row, start, shape):
    wide = jnp.where(lanes(shape) == rows(shape) + start, row, 0.0)
    return jnp.sum(wide, axis=1, keepdims=True)


def fetch(pairs, sems):
    copies = [pltpu.make_async_copy(source, target, sems.at[i]) for i, (source, target) in enumerate(pairs)]
    for copy in copies:
        copy.start()
    return copies


def pack_kernel(
    edge_in,
    send_in,
    source_in,
    surface_in,
    right_in,
    out_ref,
    rim_ref,
    edge_ref,
    send_ref,
    source_ref,
    surface_ref,
    right_ref,
    tail_ref,
    sems,
):
    blocks, width = surface_ref.shape
    rank = right_ref.shape[1]
    height = edge_ref.shape[1]
    slots, _, groups = send_ref.shape
    chips = groups // CORES
    copies = fetch(
        (
            (surface_in, surface_ref),
            (right_in, right_ref),
            (edge_in, edge_ref),
            (send_in, send_ref),
            (source_in, source_ref),
        ),
        sems,
    )
    for copy in copies:
        copy.wait()
    core = lax.rem(lax.axis_index("group"), CORES)
    every = dot_full(surface_ref[...], right_ref[...].reshape(blocks * rank, width), ((1,), (1,)))
    own = lanes((blocks, blocks * rank)) // rank == rows((blocks, blocks * rank))
    coeff = jnp.sum(jnp.where(own, every, 0.0), axis=0, keepdims=True)
    out_ref[pl.ds(0, chips, stride=ROWS), :] = jnp.broadcast_to(coeff, (chips, width))
    edge_x = edge_ref[0]
    edge_y = edge_ref[1]
    last_x = edge_x[height - 1 : height, :]
    beyond = jnp.where(lanes((1, width)) == width - 1, 0.0, pltpu.roll(last_x, width - 1, 1))
    down = last_x - beyond - edge_y[height - 1 : height, :]
    rim = jnp.where(core == CORES - 1, down, edge_y[0:1, :])
    out_ref[pl.ds(1, chips, stride=ROWS), :] = jnp.broadcast_to(rim, (chips, width))
    next_y = jnp.where(rows((height, width)) == height - 1, 0.0, pltpu.roll(edge_y, height - 1, 0))
    flow = next_y - edge_y + edge_x
    last = (lanes((8, width)) == width - 1).astype(BF16)
    first = (lanes((8, width)) == 0).astype(BF16)
    ends = jnp.concatenate(
        [
            dot_exact(last, flow, ((1,), (1,)))[0:1, :],
            dot_exact(first, edge_x, ((1,), (1,)))[0:1, :],
            jnp.broadcast_to(edge_y[0:1, width - 1 : width], (1, width - 2 * height)),
        ],
        axis=1,
    )
    own = jnp.where(core == 0, down, edge_y[0:1, :])
    rim_ref[0:blocks, :] = surface_ref[...]
    rim_ref[blocks : blocks + 1, :] = ends
    rim_ref[blocks + 1 :, :] = jnp.broadcast_to(own, (EXTRA - blocks - 1, width))
    index = jnp.concatenate(
        [send_ref[s] for s in range(slots)] + [jnp.zeros((8 - slots, groups), jnp.int32)], axis=0
    ).T
    parts = split3(edge_ref[...].reshape(2 * height, width))
    lane = lanes((groups, width))
    tail = jnp.where(lane == 2 * CORES * slots, last_x[0:1, 0:1], 0.0)
    for s in range(slots):
        column = index[:, s : s + 1]
        choice = (lanes((groups, 2 * height)) == column // width).astype(BF16)
        picked = None
        for part in parts:
            term = lax.dot_general(choice, part, (((1,), (0,)), ((), ())), preferred_element_type=F32)
            picked = term if picked is None else picked + term
        value = jnp.sum(jnp.where(lane == column % width, picked, 0.0), axis=1, keepdims=True)
        tail = jnp.where(lane == s, value, tail)
        total = jnp.zeros((groups, width), F32)
        slot = rows((groups, width)) * slots + s
        for b in range(blocks):
            total = total + jnp.where(source_ref[b : b + 1, :] == slot, surface_ref[b : b + 1, :], 0.0)
        tail = jnp.where(lane == slots + s, jnp.sum(total, axis=1, keepdims=True), tail)
    tail_ref[...] = tail
    even = tail_ref[pl.ds(0, chips, stride=CORES), :]
    odd = tail_ref[pl.ds(1, chips, stride=CORES), :]
    lane = lanes((chips, width))
    moved = pltpu.roll(odd, 2 * slots, 1)
    mine = (lane >= 2 * slots) & (lane < 2 * CORES * slots)
    out_ref[pl.ds(2, chips, stride=ROWS), :] = jnp.where(mine, moved, even)


def spread_kernel(members, slots, first_ref, rim_ref, out_ref, side_ref):
    width = rim_ref.shape[1]
    chips = first_ref.shape[0] // ROWS
    blocks = EXTRA // 2
    group = lax.axis_index("group")
    core = lax.rem(group, CORES)
    chip = group // CORES
    before = jnp.where(chip > 0, 1.0, 0.0)
    after = jnp.where(chip + 1 < chips, 1.0, 0.0)
    chip_before = lax.max(chip - 1, 0) * ROWS
    chip_after = lax.min(chip + 1, chips - 1) * ROWS
    rim_before = first_ref[pl.ds(chip_before + 1, 1), :] * before
    rim_after = first_ref[pl.ds(chip_after + 1, 1), :] * after
    corner_before = first_ref[pl.ds(chip_before + 2, 1), :] * before
    corners = 2 * CORES * slots
    lane = lanes((EXTRA, width))
    line = rows((EXTRA, width))
    rim = rim_ref[...]
    corner = jnp.where(lane < 7 * width // 8, corner_before[0:1, corners : corners + 1], rim_after[0:1, width - 1 : width])
    rim = jnp.where((line == blocks) & (lane >= 3 * width // 4), corner, rim)
    coeffs = first_ref[pl.ds(0, chips, stride=ROWS), :]
    for m in range(members):
        out_ref[m, 0:chips, :] = coeffs
        out_ref[m, chips : chips + EXTRA, :] = rim
    other = jnp.where(core == 0, rim_after, rim_before)
    side_ref[0:chips, :] = first_ref[pl.ds(2, chips, stride=ROWS), :]
    half = rows((SIDE, width)) < SIDE // 2
    side_ref[chips : chips + SIDE, :] = jnp.where(half, rim[blocks + 1 : blocks + 2, :], other)


def local_kernel(
    members,
    edge_in,
    conductance_in,
    send_in,
    source_in,
    near_columns_in,
    far_columns_in,
    far_ranks_in,
    coupling_in,
    left_in,
    side_ref,
    volume_ref,
    trace_ref,
    index_ref,
    keep_ref,
    near_pick_ref,
    coupling_ref,
    left_ref,
    edge_ref,
    conductance_ref,
    send_ref,
    source_ref,
    near_columns_ref,
    far_columns_ref,
    far_ranks_ref,
    tail_ref,
    sems,
):
    copies = fetch(
        (
            (edge_in, edge_ref),
            (conductance_in, conductance_ref),
            (send_in, send_ref),
            (source_in, source_ref),
            (near_columns_in, near_columns_ref),
            (far_columns_in, far_columns_ref),
            (far_ranks_in, far_ranks_ref),
            (left_in, left_ref),
            (coupling_in, coupling_ref),
        ),
        sems,
    )
    for copy in copies[:-2]:
        copy.wait()
    blocks, width = source_ref.shape
    height = edge_ref.shape[1]
    slots, _, groups = send_ref.shape
    chips = groups // CORES
    rank = left_ref.shape[1]
    core = lax.rem(lax.axis_index("group"), CORES)
    near_count = near_columns_ref.shape[1]
    far_count = far_columns_ref.shape[1]
    column = far_columns_ref[...]
    device = column // blocks
    group = device // members
    per_member = chips + EXTRA
    place = (group % CORES) * (members * per_member) + (device % members) * per_member + group // CORES
    index_ref[...] = jnp.zeros(index_ref.shape, jnp.int32)
    index_ref[0:blocks, 0:far_count] = place
    lane = lanes((far_count, width))
    for b in range(blocks):
        square = (far_count, far_count)
        side = lanes(square) == rows(square)
        packed = column[b : b + 1, :] % blocks * width + far_ranks_ref[b : b + 1, :]
        packed = jnp.sum(jnp.where(side, packed, 0).astype(F32), axis=1, keepdims=True).astype(jnp.int32)
        kept = (lane // rank == packed // width) & (lane % rank < packed % width)
        keep_ref[b * far_count : (b + 1) * far_count, :] = kept.astype(F32)
        square = (near_count, near_count)
        side = lanes(square) == rows(square)
        picked = jnp.where(side, near_columns_ref[b : b + 1, :], 0).astype(F32)
        picked = jnp.sum(picked, axis=1, keepdims=True).astype(jnp.int32)
        near_pick_ref[b * near_count : (b + 1) * near_count, :] = (lanes((near_count, width)) == picked).astype(F32)
    for c in range(CORES):
        half = side_ref[c, 0:chips, :]
        half = jnp.where(core == 0, half, pltpu.roll(half, width - 2 * slots, 1))
        tail_ref[pl.ds(c, chips, stride=CORES), :] = half
    tail = tail_ref[...]
    for b in range(blocks):
        trace = jnp.zeros((groups, width), F32)
        for s in range(slots):
            slot = rows((groups, width)) * slots + s
            trace = trace + jnp.where(source_ref[b : b + 1, :] == slot, tail[:, s : s + 1], 0.0)
        trace_ref[b : b + 1, :] = 0.5 * jnp.sum(trace, axis=0, keepdims=True)
    index = jnp.concatenate(
        [send_ref[s] for s in range(slots)] + [jnp.zeros((8 - slots, groups), jnp.int32)], axis=0
    ).T
    added = None
    for s in range(slots):
        column = index[:, s : s + 1]
        choice = (lanes((groups, 2 * height)) == column // width).astype(BF16)
        value = jnp.where(lanes((groups, width)) == column % width, tail[:, slots + s : slots + s + 1], 0.0)
        term = dot_exact(choice, value, ((0,), (0,)))
        added = term if added is None else added + term
    edge_x = edge_ref[0]
    edge_y = edge_ref[1]
    shape = (height, width)
    lane = lanes(shape)
    line = rows(shape)
    own = side_ref[1 - core, chips : chips + 1, :]
    other = side_ref[1 - core, chips + SIDE // 2 : chips + SIDE // 2 + 1, :]
    above = jnp.where(core == 0, other, own)
    below = jnp.where(core == 0, own, other)
    next_x = jnp.where(lane == width - 1, 0.0, pltpu.roll(edge_x, width - 1, 1))
    next_y = jnp.where(line == height - 1, below, pltpu.roll(edge_y, height - 1, 0))
    flux = next_y - edge_y - next_x + edge_x
    flux_left = jnp.where(lane == 0, -edge_x, pltpu.roll(flux, 1, 1))
    flux_up = jnp.where(line == 0, edge_y + above, pltpu.roll(flux, 1, 0))
    volume_ref[0] = flux_left - flux + conductance_ref[0] * edge_x + added[0:height, :]
    volume_ref[1] = flux_up - flux + conductance_ref[1] * edge_y + added[height : 2 * height, :]
    for copy in copies[-2:]:
        copy.wait()


def finish_kernel(
    members,
    chips,
    volume_in,
    trace_ref,
    index_in,
    keep_ref,
    near_pick_ref,
    every_ref,
    near_ref,
    coupling_ref,
    left_ref,
    volume_ref,
    surface_ref,
    index_ref,
    picked_ref,
    vector_ref,
    sem,
):
    blocks, width = trace_ref.shape
    height = volume_ref.shape[1]
    rank = left_ref.shape[1]
    per_member = chips + EXTRA
    per_core = members * per_member
    core = lax.rem(lax.axis_index("group"), CORES)
    member = lax.axis_index("member")
    copy = pltpu.make_async_copy(index_in, index_ref, sem)
    copy.start()
    near_count = near_ref.shape[1]
    far_count = coupling_ref.shape[1]
    fields = [every_ref[pl.ds(core * per_core + m * per_member + chips, EXTRA), :][0:blocks, :] for m in range(members)]
    choice = near_pick_ref[:, 0 : members * blocks].astype(BF16)
    vector_ref[...] = dot_exact(choice, jnp.concatenate(fields, axis=0), ((1,), (0,)))
    sums = []
    for b in range(blocks):
        total = jnp.zeros((width, width), F32)
        for n in range(near_count):
            at = b * near_count + n
            total = total + near_ref[b, n] * vector_ref[at : at + 1, :]
        sums.append(total)
    near = dot_exact(jnp.ones((8, width), BF16), jnp.concatenate(sums, axis=0), ((1,), (1,)))
    copy.wait()
    for b in range(blocks):
        for f in range(far_count):
            picked_ref[b * far_count + f : b * far_count + f + 1, :] = every_ref[pl.ds(index_ref[b, f], 1), :]
    picked = jnp.where(keep_ref[...] > 0.0, picked_ref[...], 0.0)
    folded = picked
    for q in range(1, width // rank):
        folded = folded + pltpu.roll(picked, q * rank, 1)
    picked_ref[...] = folded
    for b in range(blocks):
        total = jnp.zeros((rank, rank), F32)
        for f in range(far_count):
            at = b * far_count + f
            total = total + coupling_ref[b, f] * picked_ref[at : at + 1, 0:rank]
        summed = jnp.sum(total, axis=1, keepdims=True)
        far = jnp.sum(left_ref[b] * summed, axis=0, keepdims=True)
        surface_ref[b : b + 1, :] = near[0:1, b * width : (b + 1) * width] + far + trace_ref[b : b + 1, :]

    ends = chips + blocks
    before = lax.max(member - 1, 0) * per_member + ends
    after = lax.min(member + 1, members - 1) * per_member + ends
    inside = jnp.where(member > 0, 1.0, 0.0)
    mine = every_ref[pl.ds(core * per_core + before, 1), :] * inside
    theirs = every_ref[pl.ds((1 - core) * per_core + before, 1), :] * inside
    inside = jnp.where(member + 1 < members, 1.0, 0.0)
    mine_after = every_ref[pl.ds(core * per_core + after, 1), :] * inside
    theirs_after = every_ref[pl.ds((1 - core) * per_core + after, 1), :] * inside
    shape = (height, width)
    lane = lanes(shape)
    line = rows(shape)
    corner_y = 2 * height + jnp.where(core == 0, 0, 3 * height // 2)
    left = upright(mine, 0, shape)
    left = left + jnp.where(line[:, 0:1] == height - 1, upright(theirs, corner_y - height + 1, shape), 0.0)
    right = upright(mine_after, height, shape)
    corner_x = jnp.where(core == 0, 3 * height, 2 * height - 1)
    corner = jnp.sum(jnp.where(lanes((1, width)) == corner_x, theirs_after, 0.0), axis=1, keepdims=True)
    end = jnp.where(lane == width - 1, right, 0.0)
    volume_ref[0] = volume_in[0] + jnp.where(lane == 0, left, 0.0) + end
    last = jnp.where(lane == width - 1, 1.0, 0.0)
    up = jnp.where(line == 0, corner, pltpu.roll(jnp.broadcast_to(right, shape), 1, 0))
    volume_ref[1] = volume_in[1] + end - last * up


def vmem(count):
    return [pl.BlockSpec(memory_space=pltpu.VMEM)] * count


PARAMS = pltpu.CompilerParams(vmem_limit_bytes=16 * 1024 * 1024)


def body(
    edge_field,
    conductance,
    send_index,
    panel_source,
    surface_field,
    near_columns,
    near_tiles,
    far_columns,
    far_ranks,
    far_coupling,
    basis_left,
    basis_right,
):
    groups = lax.axis_size("group")
    members = lax.axis_size("member")
    slots = send_index.shape[2]
    blocks, width = surface_field.shape
    chips = groups // CORES
    send = jnp.transpose(send_index, (2, 0, 1))
    right = jnp.swapaxes(basis_right, 1, 2)
    left = jnp.swapaxes(basis_left, 1, 2)
    near_count = near_columns.shape[1]
    far_count = far_columns.shape[1]
    one_core = [[chip * CORES + core for chip in range(chips)] for core in range(CORES)]
    one_chip = [[chip * CORES + core for core in range(CORES)] for chip in range(chips)]

    hbm = pl.BlockSpec(memory_space=pltpu.HBM)
    edge_field, conductance, send, panel_source, surface_field, right, left, far_coupling = [
        pltpu.with_memory_space_constraint(array, pltpu.HBM)
        for array in (edge_field, conductance, send, panel_source, surface_field, right, left, far_coupling)
    ]
    near_columns, far_columns, far_ranks = [
        pltpu.with_memory_space_constraint(array, pltpu.HBM) for array in (near_columns, far_columns, far_ranks)
    ]

    def like(array):
        return pltpu.VMEM(array.shape, array.dtype)

    def out(*shape, dtype=F32):
        return jax.ShapeDtypeStruct(shape, dtype)

    first, rim = pl.pallas_call(
        pack_kernel,
        name="pack",
        out_shape=(out(chips * ROWS, width), out(EXTRA, width)),
        in_specs=[hbm] * 5,
        out_specs=tuple(vmem(2)),
        scratch_shapes=[
            like(edge_field),
            like(send),
            like(panel_source),
            like(surface_field),
            like(right),
            pltpu.VMEM((groups, width), F32),
            pltpu.SemaphoreType.DMA((5,)),
        ],
        compiler_params=PARAMS,
    )(edge_field, send, panel_source, surface_field, right)
    first = lax.all_to_all(
        first.reshape(chips, 1, ROWS * width),
        "group",
        split_axis=0,
        concat_axis=0,
        axis_index_groups=one_core,
        tiled=True,
    ).reshape(chips * ROWS, width)
    second, side = pl.pallas_call(
        functools.partial(spread_kernel, members, slots),
        name="spread",
        out_shape=(out(members, chips + EXTRA, width), out(chips + SIDE, width)),
        in_specs=vmem(2),
        out_specs=tuple(vmem(2)),
        compiler_params=PARAMS,
    )(first, rim)
    second = lax.all_to_all(second, "member", split_axis=0, concat_axis=0, tiled=True)
    side = lax.all_gather(side, "group", axis=0, axis_index_groups=one_chip, tiled=True)
    volume, trace, index, keep, near_pick, coupling, left = pl.pallas_call(
        functools.partial(local_kernel, members),
        name="local",
        out_shape=(
            out(*edge_field.shape),
            out(blocks, width),
            out(8, width, dtype=jnp.int32),
            out(blocks * far_count, width),
            out(blocks * near_count, width),
            out(*far_coupling.shape),
            out(*left.shape),
        ),
        in_specs=[hbm] * 9 + vmem(1),
        out_specs=tuple(vmem(7)),
        scratch_shapes=[
            like(edge_field),
            like(conductance),
            like(send),
            like(panel_source),
            like(near_columns),
            like(far_columns),
            like(far_ranks),
            pltpu.VMEM((groups, width), F32),
            pltpu.SemaphoreType.DMA((9,)),
        ],
        compiler_params=PARAMS,
        cost_estimate=pl.CostEstimate(flops=10_000_000, bytes_accessed=2_500_000, transcendentals=0),
    )(
        edge_field,
        conductance,
        send,
        panel_source,
        near_columns,
        far_columns,
        far_ranks,
        far_coupling,
        left,
        side.reshape(CORES, chips + SIDE, width),
    )
    every = lax.all_gather(
        second.reshape(members * (chips + EXTRA), width),
        "group",
        axis=0,
        axis_index_groups=one_chip,
        tiled=True,
    )
    return pl.pallas_call(
        functools.partial(finish_kernel, members, chips),
        name="finish",
        out_shape=(out(*edge_field.shape), out(blocks, width)),
        in_specs=vmem(9),
        out_specs=tuple(vmem(2)),
        scratch_shapes=[
            pltpu.SMEM((8, width), jnp.int32),
            pltpu.VMEM((blocks * far_count, width), F32),
            pltpu.VMEM((blocks * near_count, width), F32),
            pltpu.SemaphoreType.DMA,
        ],
        compiler_params=PARAMS,
    )(volume, trace, index, keep, near_pick, every, near_tiles, coupling, left)


def solution(mesh):
    both = ("group", "member")
    placed = (
        P(None, "group", "member"),
        P(None, "group", "member"),
        P(both, None, None),
        P(both, None),
        P(both, None),
        P(both, None),
        P(both, None, None, None),
        P(both, None),
        P(both, None),
        P(both, None, None, None),
        P(both, None, None),
        P(both, None, None),
    )
    return jax.shard_map(
        body,
        mesh=mesh,
        in_specs=placed,
        out_specs=(P(None, "group", "member"), P(both, None)),
        check_vma=False,
    )
```

time: 217 us -> 55.7 us (0.26)
  blocking collectives: 124 us -> 38.9 us
  starting transfers between devices: 52.3 us -> 6.82 us
  other arithmetic: 12 us -> 0 us
  local copies, waits for them, and re-layouts: 11.9 us -> 0.01 us
  waiting for transfers between devices: 10.8 us -> 3.33 us
  Pallas kernels: 0 us -> 5.7 us
  matrix products: 4.41 us -> 0 us
    all_gather x2, blocking collectives: 124 us -> 9.09 us  [the longest x1 5.15 us: body(): lax.all_gather(second.reshape(members * (chips + EXTRA), width), 'group',...]
    all_to_all x0 -> x1, blocking collectives: none -> 29.8 us  [body(): lax.all_to_all(first.reshape(chips, 1, ROWS * width), 'group', split_axis...]
    all_to_all x2 -> x1, starting transfers between devices: 34.4 us -> 6.82 us  [body(): lax.all_to_all(second, 'member', split_axis=0, concat_axis=0, tiled=True)]
    ppermute x4 -> x0, starting transfers between devices: 18 us -> none  [the longest x2 10.5 us: padded_2(): lax.ppermute(head, axis, [((i + 1) % count, i) for i in range(ends)])]
    gather x4 -> x0, local copies, waits for them, and re-layouts: 7.8 us -> none  [the longest x1 3.49 us: body(): trace = received.reshape(-1)[panel_source]]
    scatter-add x2 -> x0, other arithmetic: 7.53 us -> none  [the longest x1 4.23 us: body(): jax.ops.segment_sum(surface_field.reshape(-1), panel_source.reshape(-1),...]
    all_to_all x2 -> x1, waiting for transfers between devices: 10.7 us -> 3.33 us  [body(): lax.all_to_all(second, 'member', split_axis=0, concat_axis=0, tiled=True)]
    pallas_call x0 -> x4, Pallas kernels: none -> 5.7 us  [the longest x1 1.76 us: body(): pl.pallas_call(functools.partial(local_kernel, members), name='local', ou...]
  transfers between devices with their start and end apart: 6 -> 1, of which waited for: 1 -> 1; matrix products, arithmetic and copies ran while one was open for 8% -> 0% of each run, Pallas kernels for 0% -> 3%
where the time goes in v3:
time: 55.7 us; the launch traced here: 55.4 us
  blocking collectives  38.9 us (70%)
  starting transfers between devices  6.82 us (12%)
  Pallas kernels  5.7 us (10%)
  waiting for transfers between devices  3.33 us (6%)
  between operations  0.65 us (1%)
    all_to_all x1, blocking collectives, body(): lax.all_to_all(first.reshape(chips, 1, ROWS * width), 'group', split_axis...  29.8 us
    all_to_all x1, starting transfers between devices, body(): lax.all_to_all(second, 'member', split_axis=0, concat_axis=0, tiled=True)  6.82 us
    all_gather x1, blocking collectives, body(): lax.all_gather(second.reshape(members * (chips + EXTRA), width), 'group',...  5.15 us
    all_gather x1, blocking collectives, body(): lax.all_gather(side, 'group', axis=0, axis_index_groups=one_chip, tiled=T...  3.94 us
    all_to_all x1, waiting for transfers between devices, body(): lax.all_to_all(second, 'member', split_axis=0, concat_axis=0, tiled=True)  3.33 us
    pallas_call x1, Pallas kernels, body(): pl.pallas_call(functools.partial(local_kernel, members), name='local', ou...  1.76 us
    pallas_call x1, Pallas kernels, body(): pl.pallas_call(pack_kernel, name='pack', out_shape=(out(chips * ROWS, wid...  1.6 us
    pallas_call x1, Pallas kernels, body(): pl.pallas_call(functools.partial(finish_kernel, members, chips), name='fi...  1.53 us
  transfers between devices with their start and end apart: 1, of which 1 were waited for; matrix products, arithmetic and copies ran while one was open for 0% of the time, Pallas kernels for 3%

profile of v3, /device:TPU:1, one launch (start us, length us, event | category | flops | bytes accessed | tf_op | source)
XLA Modules:
  0.0 55.4 jit_solution(8196333468521905061)
XLA Ops:
  0.6 1.6 %pack.1 = (f32[144,128]{1,0:T(8,128)S(1)}, f32[8,128]{1,0:T(8,128)S(1)}) custom-call(f32[2,32,128]{2,1,0:T(8,128)} %edge_in.3, s32[5,1,96]{2,1,0:T(1,128)} %bitcast.13, s32[4,128]{1,0:T(4,128)} %source_in.3, f32[4,128]{1,0:T(4,128)} %surface_in.1, f32[4,32,128]{2,1,0:T(8,128)} %bitcast.12), custom_call_target="tpu_custom_call" | custom-call | tf_op jit(solution)/shard_map/pack/pallas_call | solution.py:426
  2.2 29.8 %all_to_all.10 = f32[48,1,384]{2,1,0:T(1,128)S(1)} all-to-all(f32[48,1,384]{2,1,0:T(1,128)S(1)} %bitcast.9), channel_id=1, replica_groups={{0,16,32,48,64,80,96,112,128,144,160,176,192,208,224,240,256,272,288,30..., dimensions={0} | all-to-all | bytes 147456 | tf_op jit(solution)/shard_map/all_to_all | solution.py:443
  32.0 0.8 %spread.1 = (f32[8,56,128]{2,1,0:T(8,128)}, f32[56,128]{1,0:T(8,128)S(1)}) custom-call(f32[144,128]{1,0:T(8,128)S(1)} %bitcast.7, f32[8,128]{1,0:T(8,128)S(1)} %get-tuple-element.14.rim_ref), custom_call_target="tpu_custom_call" | custom-call | tf_op jit(solution)/shard_map/spread/pallas_call | solution.py:451
  32.8 6.8 %all-to-all-start.1 = ((f32[8,56,128]{2,1,0:T(8,128)}), f32[8,56,128]{2,1,0:T(8,128)S(1)}, u32[]{:S(2)}, u32[]{:S(2)}) async-start(f32[8,56,128]{2,1,0:T(8,128)} %get-tuple-element.21), calls=%async_computation.1 | async-start | bytes 458752 | tf_op jit(solution)/shard_map/all_to_all | solution.py:459
  39.7 0.0 copy-start
  39.7 3.9 %all_gather.6 = f32[112,128]{1,0:T(8,128)S(1)} all-gather(f32[56,128]{1,0:T(8,128)S(1)} %get-tuple-element.15), channel_id=1, replica_groups={{0,8},{16,24},{32,40},{48,56},{64,72},{80,88},{96,104},{112,120},{128,1..., dimensions={0}, use_global_device_ids=true | all-gather | bytes 86016 | tf_op jit(solution)/shard_map/all_gather | solution.py:460
  43.6 1.8 %local.1 = (f32[2,32,128]{2,1,0:T(8,128)S(1)}, f32[4,128]{1,0:T(4,128)S(1)}, s32[8,128]{1,0:T(8,128)S(1)}, f32[64,128]{1,0:T(8,128)S(1)}, f32[16,128]{1,0:T(8,12...) custom-call(f32[2,32,128]{2,1,0:T(8,128)} %edge_in.3, f32[2,32,128]{2,1,0:T(8,128)} %conductance_in.1, ...), custom_call_target="tpu_custom_call" | custom-call | flops 10000000 | bytes 2500000 | tf_op jit(solution)/shard_map/local/pallas_call | solution.py:461
  45.4 3.3 %all-to-all-done.1 = f32[8,56,128]{2,1,0:T(8,128)S(1)} async-done(((f32[8,56,128]{2,1,0:T(8,128)}), f32[8,56,128]{2,1,0:T(8,128)S(1)}, u32[]{:S(2)}, u32[]{:S(2)}) %all-to-all-start.1) | async-done | bytes 229408 | tf_op jit(solution)/shard_map/all_to_all | solution.py:459
  48.7 5.1 %all_gather.7.every_ref = f32[896,128]{1,0:T(8,128)S(1)} all-gather(f32[448,128]{1,0:T(8,128)S(1)} %bitcast.10), channel_id=1, replica_groups={{0,8},{16,24},{32,40},{48,56},{64,72},{80,88},{96,104},{112,120},{128,1..., dimensions={0}, use_global_device_ids=true | all-gather | bytes 688128 | tf_op jit(solution)/shard_map/all_gather | solution.py:500
  53.9 0.0 copy-done
  53.9 1.5 %finish.1 = (f32[2,32,128]{2,1,0:T(8,128)}, f32[4,128]{1,0:T(4,128)}) custom-call(f32[2,32,128]{2,1,0:T(8,128)S(1)} %get-tuple-element.16.volume_in, f32[4,128]{1,0:T(4,128)S(1)} %get-tuple-element.17.trace_ref, s32[8,128]{1,0:T(8,128)S(1)} %get-tuple-element.18.index_in, f32[64,128]{1,0:T(8,128)S(1)} %get-tuple-element.19.keep_ref, ...), custom_call_target="tpu_custom_call" | custom-call | tf_op jit(solution)/shard_map/finish/pallas_call | solution.py:507
Async XLA Ops:
  32.8 15.9 %all-to-all-start.1 = ((f32[8,56,128]{2,1,0:T(8,128)}), f32[8,56,128]{2,1,0:T(8,128)S(1)}, u32[]{:S(2)}, u32[]{:S(2)}) async-start(f32[8,56,128]{2,1,0:T(8,128)} %get-tuple-element.21), calls=%async_computation.1 | async-start | bytes 458752 | tf_op jit(solution)/shard_map/all_to_all | solution.py:459
  39.7 14.2 %copy-start = (f32[4,4,128,128]{3,2,1,0:T(8,128)S(1)}, f32[4,4,128,128]{3,2,1,0:T(8,128)}, u32[]{:S(2)}) copy-start(f32[4,4,128,128]{3,2,1,0:T(8,128)} %near_ref.1) | copy-start | bytes 3145732

commit v4 on v3

--- a/solution.py
+++ b/solution.py
@@ -12,7 +12,6 @@
 HIGHEST = lax.Precision.HIGHEST
 CORES = 2
 ROWS = 3
-EXTRA = 8
 SIDE = 8
 
 
@@ -54,6 +53,12 @@
     for copy in copies:
         copy.start()
     return copies
+
+
+def slot_columns(send_ref):
+    slots, _, groups = send_ref.shape
+    rest = jnp.zeros((8 - slots, groups), jnp.int32)
+    return jnp.concatenate([send_ref[s] for s in range(slots)] + [rest], axis=0).T
 
 
 def pack_kernel(
@@ -77,30 +82,29 @@
     height = edge_ref.shape[1]
     slots, _, groups = send_ref.shape
     chips = groups // CORES
+    bits = width.bit_length() - 1
     copies = fetch(
         (
-            (surface_in, surface_ref),
-            (right_in, right_ref),
             (edge_in, edge_ref),
             (send_in, send_ref),
+            (surface_in, surface_ref),
             (source_in, source_ref),
+            (right_in, right_ref),
         ),
         sems,
     )
-    for copy in copies:
+    core = lax.rem(lax.axis_index("group"), CORES)
+    for copy in copies[:2]:
         copy.wait()
-    core = lax.rem(lax.axis_index("group"), CORES)
-    every = dot_full(surface_ref[...], right_ref[...].reshape(blocks * rank, width), ((1,), (1,)))
-    own = lanes((blocks, blocks * rank)) // rank == rows((blocks, blocks * rank))
-    coeff = jnp.sum(jnp.where(own, every, 0.0), axis=0, keepdims=True)
-    out_ref[pl.ds(0, chips, stride=ROWS), :] = jnp.broadcast_to(coeff, (chips, width))
+    for copy in copies[2:]:
+        copy.wait()
     edge_x = edge_ref[0]
     edge_y = edge_ref[1]
     last_x = edge_x[height - 1 : height, :]
     beyond = jnp.where(lanes((1, width)) == width - 1, 0.0, pltpu.roll(last_x, width - 1, 1))
     down = last_x - beyond - edge_y[height - 1 : height, :]
     rim = jnp.where(core == CORES - 1, down, edge_y[0:1, :])
-    out_ref[pl.ds(1, chips, stride=ROWS), :] = jnp.broadcast_to(rim, (chips, width))
+    own = jnp.where(core == 0, down, edge_y[0:1, :])
     next_y = jnp.where(rows((height, width)) == height - 1, 0.0, pltpu.roll(edge_y, height - 1, 0))
     flow = next_y - edge_y + edge_x
     last = (lanes((8, width)) == width - 1).astype(BF16)
@@ -113,43 +117,47 @@
         ],
         axis=1,
     )
-    own = jnp.where(core == 0, down, edge_y[0:1, :])
-    rim_ref[0:blocks, :] = surface_ref[...]
-    rim_ref[blocks : blocks + 1, :] = ends
-    rim_ref[blocks + 1 :, :] = jnp.broadcast_to(own, (EXTRA - blocks - 1, width))
-    index = jnp.concatenate(
-        [send_ref[s] for s in range(slots)] + [jnp.zeros((8 - slots, groups), jnp.int32)], axis=0
-    ).T
+    index = slot_columns(send_ref)
     parts = split3(edge_ref[...].reshape(2 * height, width))
     lane = lanes((groups, width))
     tail = jnp.where(lane == 2 * CORES * slots, last_x[0:1, 0:1], 0.0)
     for s in range(slots):
-        column = index[:, s : s + 1]
-        choice = (lanes((groups, 2 * height)) == column // width).astype(BF16)
+        column = jnp.broadcast_to(index[:, s : s + 1], (groups, width))
+        choice = (lanes((groups, 2 * height)) == (column >> bits)[:, 0 : 2 * height]).astype(BF16)
         picked = None
         for part in parts:
             term = lax.dot_general(choice, part, (((1,), (0,)), ((), ())), preferred_element_type=F32)
             picked = term if picked is None else picked + term
-        value = jnp.sum(jnp.where(lane == column % width, picked, 0.0), axis=1, keepdims=True)
+        value = jnp.sum(jnp.where(lane == (column & (width - 1)), picked, 0.0), axis=1, keepdims=True)
         tail = jnp.where(lane == s, value, tail)
+    slot = rows((groups, width)) * slots
+    for s in range(slots):
         total = jnp.zeros((groups, width), F32)
-        slot = rows((groups, width)) * slots + s
         for b in range(blocks):
-            total = total + jnp.where(source_ref[b : b + 1, :] == slot, surface_ref[b : b + 1, :], 0.0)
+            total = total + jnp.where(source_ref[b : b + 1, :] - s == slot, surface_ref[b : b + 1, :], 0.0)
         tail = jnp.where(lane == slots + s, jnp.sum(total, axis=1, keepdims=True), tail)
+    every = dot_full(surface_ref[...], right_ref[...].reshape(blocks * rank, width), ((1,), (1,)))
+    mine = lanes((blocks, blocks * rank)) // rank == rows((blocks, blocks * rank))
+    coeff = jnp.sum(jnp.where(mine, every, 0.0), axis=0, keepdims=True)
+    out_ref[pl.ds(0, chips, stride=ROWS), :] = jnp.broadcast_to(coeff, (chips, width))
+    out_ref[pl.ds(1, chips, stride=ROWS), :] = jnp.broadcast_to(rim, (chips, width))
     tail_ref[...] = tail
     even = tail_ref[pl.ds(0, chips, stride=CORES), :]
     odd = tail_ref[pl.ds(1, chips, stride=CORES), :]
     lane = lanes((chips, width))
     moved = pltpu.roll(odd, 2 * slots, 1)
-    mine = (lane >= 2 * slots) & (lane < 2 * CORES * slots)
-    out_ref[pl.ds(2, chips, stride=ROWS), :] = jnp.where(mine, moved, even)
-
-
-def spread_kernel(members, slots, first_ref, rim_ref, out_ref, side_ref):
+    theirs = (lane >= 2 * slots) & (lane < 2 * CORES * slots)
+    out_ref[pl.ds(2, chips, stride=ROWS), :] = jnp.where(theirs, moved, even)
+    rim_ref[0:blocks, :] = surface_ref[...]
+    rim_ref[blocks : blocks + 1, :] = ends
+    rim_ref[blocks + 1 : blocks + 2, :] = own
+
+
+def spread_kernel(members, slots, first_ref, rim_ref, out_ref, side_ref, block_ref):
     width = rim_ref.shape[1]
     chips = first_ref.shape[0] // ROWS
-    blocks = EXTRA // 2
+    blocks = rim_ref.shape[0] - 2
+    per_member = chips + blocks + 1
     group = lax.axis_index("group")
     core = lax.rem(group, CORES)
     chip = group // CORES
@@ -161,19 +169,19 @@
     rim_after = first_ref[pl.ds(chip_after + 1, 1), :] * after
     corner_before = first_ref[pl.ds(chip_before + 2, 1), :] * before
     corners = 2 * CORES * slots
-    lane = lanes((EXTRA, width))
-    line = rows((EXTRA, width))
-    rim = rim_ref[...]
-    corner = jnp.where(lane < 7 * width // 8, corner_before[0:1, corners : corners + 1], rim_after[0:1, width - 1 : width])
-    rim = jnp.where((line == blocks) & (lane >= 3 * width // 4), corner, rim)
-    coeffs = first_ref[pl.ds(0, chips, stride=ROWS), :]
+    lane = lanes((1, width))
+    ends = rim_ref[blocks : blocks + 1, :]
+    ends = jnp.where(lane >= 3 * width // 4, corner_before[:, corners : corners + 1], ends)
+    ends = jnp.where(lane >= 7 * width // 8, rim_after[:, width - 1 : width], ends)
+    block_ref[0:chips, :] = first_ref[pl.ds(0, chips, stride=ROWS), :]
+    block_ref[chips : chips + blocks, :] = rim_ref[0:blocks, :]
+    block_ref[chips + blocks : chips + blocks + 1, :] = ends
     for m in range(members):
-        out_ref[m, 0:chips, :] = coeffs
-        out_ref[m, chips : chips + EXTRA, :] = rim
+        out_ref[m * per_member : (m + 1) * per_member, :] = block_ref[...]
     other = jnp.where(core == 0, rim_after, rim_before)
     side_ref[0:chips, :] = first_ref[pl.ds(2, chips, stride=ROWS), :]
     half = rows((SIDE, width)) < SIDE // 2
-    side_ref[chips : chips + SIDE, :] = jnp.where(half, rim[blocks + 1 : blocks + 2, :], other)
+    side_ref[chips : chips + SIDE, :] = jnp.where(half, rim_ref[blocks + 1 : blocks + 2, :], other)
 
 
 def local_kernel(
@@ -232,10 +240,10 @@
     column = far_columns_ref[...]
     device = column // blocks
     group = device // members
-    per_member = chips + EXTRA
+    per_member = chips + blocks + 1
     place = (group % CORES) * (members * per_member) + (device % members) * per_member + group // CORES
-    index_ref[...] = jnp.zeros(index_ref.shape, jnp.int32)
-    index_ref[0:blocks, 0:far_count] = place
+    rest = jnp.zeros((1, width - blocks * far_count), jnp.int32)
+    index_ref[...] = jnp.concatenate([place[b : b + 1, :] for b in range(blocks)] + [rest], axis=1)
     lane = lanes((far_count, width))
     for b in range(blocks):
         square = (far_count, far_count)
@@ -254,20 +262,19 @@
         half = jnp.where(core == 0, half, pltpu.roll(half, width - 2 * slots, 1))
         tail_ref[pl.ds(c, chips, stride=CORES), :] = half
     tail = tail_ref[...]
+    slot = rows((groups, width)) * slots
     for b in range(blocks):
         trace = jnp.zeros((groups, width), F32)
         for s in range(slots):
-            slot = rows((groups, width)) * slots + s
-            trace = trace + jnp.where(source_ref[b : b + 1, :] == slot, tail[:, s : s + 1], 0.0)
+            trace = trace + jnp.where(source_ref[b : b + 1, :] - s == slot, tail[:, s : s + 1], 0.0)
         trace_ref[b : b + 1, :] = 0.5 * jnp.sum(trace, axis=0, keepdims=True)
-    index = jnp.concatenate(
-        [send_ref[s] for s in range(slots)] + [jnp.zeros((8 - slots, groups), jnp.int32)], axis=0
-    ).T
+    index = slot_columns(send_ref)
+    bits = width.bit_length() - 1
     added = None
     for s in range(slots):
-        column = index[:, s : s + 1]
-        choice = (lanes((groups, 2 * height)) == column // width).astype(BF16)
-        value = jnp.where(lanes((groups, width)) == column % width, tail[:, slots + s : slots + s + 1], 0.0)
+        column = jnp.broadcast_to(index[:, s : s + 1], (groups, width))
+        choice = (lanes((groups, 2 * height)) == (column >> bits)[:, 0 : 2 * height]).astype(BF16)
+        value = jnp.where(lanes((groups, width)) == (column & (width - 1)), tail[:, slots + s : slots + s + 1], 0.0)
         term = dot_exact(choice, value, ((0,), (0,)))
         added = term if added is None else added + term
     edge_x = edge_ref[0]
@@ -295,7 +302,7 @@
     chips,
     volume_in,
     trace_ref,
-    index_in,
+    index_ref,
     keep_ref,
     near_pick_ref,
     every_ref,
@@ -304,23 +311,19 @@
     left_ref,
     volume_ref,
     surface_ref,
-    index_ref,
     picked_ref,
     vector_ref,
-    sem,
 ):
     blocks, width = trace_ref.shape
     height = volume_ref.shape[1]
     rank = left_ref.shape[1]
-    per_member = chips + EXTRA
+    per_member = chips + blocks + 1
     per_core = members * per_member
     core = lax.rem(lax.axis_index("group"), CORES)
     member = lax.axis_index("member")
-    copy = pltpu.make_async_copy(index_in, index_ref, sem)
-    copy.start()
     near_count = near_ref.shape[1]
     far_count = coupling_ref.shape[1]
-    fields = [every_ref[pl.ds(core * per_core + m * per_member + chips, EXTRA), :][0:blocks, :] for m in range(members)]
+    fields = [every_ref[pl.ds(core * per_core + m * per_member + chips, blocks), :] for m in range(members)]
     choice = near_pick_ref[:, 0 : members * blocks].astype(BF16)
     vector_ref[...] = dot_exact(choice, jnp.concatenate(fields, axis=0), ((1,), (0,)))
     sums = []
@@ -331,10 +334,10 @@
             total = total + near_ref[b, n] * vector_ref[at : at + 1, :]
         sums.append(total)
     near = dot_exact(jnp.ones((8, width), BF16), jnp.concatenate(sums, axis=0), ((1,), (1,)))
-    copy.wait()
     for b in range(blocks):
         for f in range(far_count):
-            picked_ref[b * far_count + f : b * far_count + f + 1, :] = every_ref[pl.ds(index_ref[b, f], 1), :]
+            at = b * far_count + f
+            picked_ref[at : at + 1, :] = every_ref[pl.ds(index_ref[0, at], 1), :]
     picked = jnp.where(keep_ref[...] > 0.0, picked_ref[...], 0.0)
     folded = picked
     for q in range(1, width // rank):
@@ -400,6 +403,7 @@
     slots = send_index.shape[2]
     blocks, width = surface_field.shape
     chips = groups // CORES
+    per_member = chips + blocks + 1
     send = jnp.transpose(send_index, (2, 0, 1))
     right = jnp.swapaxes(basis_right, 1, 2)
     left = jnp.swapaxes(basis_left, 1, 2)
@@ -426,7 +430,7 @@
     first, rim = pl.pallas_call(
         pack_kernel,
         name="pack",
-        out_shape=(out(chips * ROWS, width), out(EXTRA, width)),
+        out_shape=(out(chips * ROWS, width), out(blocks + 2, width)),
         in_specs=[hbm] * 5,
         out_specs=tuple(vmem(2)),
         scratch_shapes=[
@@ -451,12 +455,15 @@
     second, side = pl.pallas_call(
         functools.partial(spread_kernel, members, slots),
         name="spread",
-        out_shape=(out(members, chips + EXTRA, width), out(chips + SIDE, width)),
+        out_shape=(out(members * per_member, width), out(chips + SIDE, width)),
         in_specs=vmem(2),
         out_specs=tuple(vmem(2)),
+        scratch_shapes=[pltpu.VMEM((per_member, width), F32)],
         compiler_params=PARAMS,
     )(first, rim)
-    second = lax.all_to_all(second, "member", split_axis=0, concat_axis=0, tiled=True)
+    second = lax.all_to_all(
+        second.reshape(members, 1, per_member * width), "member", split_axis=0, concat_axis=0, tiled=True
+    )
     side = lax.all_gather(side, "group", axis=0, axis_index_groups=one_chip, tiled=True)
     volume, trace, index, keep, near_pick, coupling, left = pl.pallas_call(
         functools.partial(local_kernel, members),
@@ -464,7 +471,7 @@
         out_shape=(
             out(*edge_field.shape),
             out(blocks, width),
-            out(8, width, dtype=jnp.int32),
+            out(1, width, dtype=jnp.int32),
             out(blocks * far_count, width),
             out(blocks * near_count, width),
             out(*far_coupling.shape),
@@ -498,7 +505,7 @@
         side.reshape(CORES, chips + SIDE, width),
     )
     every = lax.all_gather(
-        second.reshape(members * (chips + EXTRA), width),
+        second.reshape(members * per_member, width),
         "group",
         axis=0,
         axis_index_groups=one_chip,
@@ -511,10 +518,8 @@
         in_specs=vmem(9),
         out_specs=tuple(vmem(2)),
         scratch_shapes=[
-            pltpu.SMEM((8, width), jnp.int32),
             pltpu.VMEM((blocks * far_count, width), F32),
             pltpu.VMEM((blocks * near_count, width), F32),
-            pltpu.SemaphoreType.DMA,
         ],
         compiler_params=PARAMS,
     )(volume, trace, index, keep, near_pick, every, near_tiles, coupling, left)

time: 55.7 us -> 55.1 us (0.989)
  no operation moved by 1% of the time
where the time goes in v4:
time: 55.1 us; the launch traced here: 54.8 us
  blocking collectives  38.9 us (71%)
  starting transfers between devices  6.82 us (12%)
  Pallas kernels  5.25 us (10%)
  waiting for transfers between devices  3.15 us (6%)
  between operations  0.65 us (1%)
    all_to_all x1, blocking collectives, body(): lax.all_to_all(first.reshape(chips, 1, ROWS * width), 'group', split_axis...  29.8 us
    all_to_all x1, starting transfers between devices, body(): lax.all_to_all(second.reshape(members, 1, per_member * width), 'member',...  6.82 us
    all_gather x1, blocking collectives, body(): lax.all_gather(second.reshape(members * per_member, width), 'group', axis...  5.14 us
    all_gather x1, blocking collectives, body(): lax.all_gather(side, 'group', axis=0, axis_index_groups=one_chip, tiled=T...  3.94 us
    all_to_all x1, waiting for transfers between devices, body(): lax.all_to_all(second.reshape(members, 1, per_member * width), 'member',...  3.15 us
    pallas_call x1, Pallas kernels, body(): pl.pallas_call(functools.partial(local_kernel, members), name='local', ou...  1.8 us
    pallas_call x1, Pallas kernels, body(): pl.pallas_call(pack_kernel, name='pack', out_shape=(out(chips * ROWS, wid...  1.56 us
    pallas_call x1, Pallas kernels, body(): pl.pallas_call(functools.partial(finish_kernel, members, chips), name='fi...  1.13 us
  transfers between devices with their start and end apart: 1, of which 1 were waited for; matrix products, arithmetic and copies ran while one was open for 0% of the time, Pallas kernels for 3%

profile of v4, /device:TPU:1, one launch (start us, length us, event | category | flops | bytes accessed | tf_op | source)
XLA Modules:
  0.0 54.8 jit_solution(6921736802482583416)
XLA Ops:
  0.6 1.6 %pack.1 = (f32[144,128]{1,0:T(8,128)S(1)}, f32[6,128]{1,0:T(8,128)S(1)}) custom-call(f32[2,32,128]{2,1,0:T(8,128)} %edge_in.3, s32[5,1,96]{2,1,0:T(1,128)} %bitcast.14, s32[4,128]{1,0:T(4,128)} %source_in.3, f32[4,128]{1,0:T(4,128)} %surface_in.1, f32[4,32,128]{2,1,0:T(8,128)} %bitcast.13), custom_call_target="tpu_custom_call" | custom-call | tf_op jit(solution)/shard_map/pack/pallas_call | solution.py:430
  2.2 29.8 %all_to_all.10 = f32[48,1,384]{2,1,0:T(1,128)S(1)} all-to-all(f32[48,1,384]{2,1,0:T(1,128)S(1)} %bitcast.10), channel_id=1, replica_groups={{0,16,32,48,64,80,96,112,128,144,160,176,192,208,224,240,256,272,288,30..., dimensions={0} | all-to-all | bytes 147456 | tf_op jit(solution)/shard_map/all_to_all | solution.py:447
  32.0 0.8 %spread.1 = (f32[424,128]{1,0:T(8,128)}, f32[56,128]{1,0:T(8,128)S(1)}) custom-call(f32[144,128]{1,0:T(8,128)S(1)} %bitcast.8, f32[6,128]{1,0:T(8,128)S(1)} %get-tuple-element.14.rim_ref), custom_call_target="tpu_custom_call" | custom-call | tf_op jit(solution)/shard_map/spread/pallas_call | solution.py:455
  32.8 6.8 %all-to-all-start.1 = ((f32[8,1,6784]{2,1,0:T(1,128)}), f32[8,1,6784]{2,1,0:T(1,128)S(1)}, u32[]{:S(2)}, u32[]{:S(2)}) async-start(f32[8,1,6784]{2,1,0:T(1,128)} %bitcast.6), calls=%async_computation.1 | async-start | bytes 434176 | tf_op jit(solution)/shard_map/all_to_all | solution.py:464
  39.6 0.0 copy-start
  39.6 3.9 %all_gather.6 = f32[112,128]{1,0:T(8,128)S(1)} all-gather(f32[56,128]{1,0:T(8,128)S(1)} %get-tuple-element.15), channel_id=1, replica_groups={{0,8},{16,24},{32,40},{48,56},{64,72},{80,88},{96,104},{112,120},{128,1..., dimensions={0}, use_global_device_ids=true | all-gather | bytes 86016 | tf_op jit(solution)/shard_map/all_gather | solution.py:467
  43.5 1.8 %local.1 = (f32[2,32,128]{2,1,0:T(8,128)S(1)}, f32[4,128]{1,0:T(4,128)S(1)}, s32[1,128]{1,0:T(1,128)S(1)}, f32[64,128]{1,0:T(8,128)S(1)}, f32[16,128]{1,0:T(8,12...) custom-call(f32[2,32,128]{2,1,0:T(8,128)} %edge_in.3, f32[2,32,128]{2,1,0:T(8,128)} %conductance_in.1, ...), custom_call_target="tpu_custom_call" | custom-call | flops 10000000 | bytes 2500000 | tf_op jit(solution)/shard_map/local/pallas_call | solution.py:468
  45.3 3.2 %all-to-all-done.1 = f32[8,1,6784]{2,1,0:T(1,128)S(1)} async-done(((f32[8,1,6784]{2,1,0:T(1,128)}), f32[8,1,6784]{2,1,0:T(1,128)S(1)}, u32[]{:S(2)}, u32[]{:S(2)}) %all-to-all-start.1) | async-done | bytes 217120 | tf_op jit(solution)/shard_map/all_to_all | solution.py:464
  48.5 5.1 %all_gather.7.every_ref = f32[848,128]{1,0:T(8,128)S(1)} all-gather(f32[424,128]{1,0:T(8,128)S(1)} %bitcast.11), channel_id=1, replica_groups={{0,8},{16,24},{32,40},{48,56},{64,72},{80,88},{96,104},{112,120},{128,1..., dimensions={0}, use_global_device_ids=true | all-gather | bytes 651264 | tf_op jit(solution)/shard_map/all_gather | solution.py:507
  53.6 0.0 copy-done
  53.6 1.1 %finish.1 = (f32[2,32,128]{2,1,0:T(8,128)}, f32[4,128]{1,0:T(4,128)}) custom-call(f32[2,32,128]{2,1,0:T(8,128)S(1)} %get-tuple-element.16.volume_in, f32[4,128]{1,0:T(4,128)S(1)} %get-tuple-element.17.trace_ref, s32[1,128]{1,0:T(1,128)S(1)} %get-tuple-element.18.index_ref, f32[64,128]{1,0:T(8,128)S(1)} %get-tuple-element.19.keep_ref, ...), custom_call_target="tpu_custom_call" | custom-call | tf_op jit(solution)/shard_map/finish/pallas_call | solution.py:514
Async XLA Ops:
  32.8 15.7 %all-to-all-start.1 = ((f32[8,1,6784]{2,1,0:T(1,128)}), f32[8,1,6784]{2,1,0:T(1,128)S(1)}, u32[]{:S(2)}, u32[]{:S(2)}) async-start(f32[8,1,6784]{2,1,0:T(1,128)} %bitcast.6), calls=%async_computation.1 | async-start | bytes 434176 | tf_op jit(solution)/shard_map/all_to_all | solution.py:464
  39.6 14.0 %copy-start = (f32[4,4,128,128]{3,2,1,0:T(8,128)S(1)}, f32[4,4,128,128]{3,2,1,0:T(8,128)}, u32[]{:S(2)}) copy-start(f32[4,4,128,128]{3,2,1,0:T(8,128)} %near_ref.1) | copy-start | bytes 3145732

commit v5 on v4

--- a/solution.py
+++ b/solution.py
@@ -46,6 +46,10 @@
 def upright(row, start, shape):
     wide = jnp.where(lanes(shape) == rows(shape) + start, row, 0.0)
     return jnp.sum(wide, axis=1, keepdims=True)
+
+
+def side_of(member, members):
+    return 2 * member // members
 
 
 def fetch(pairs, sems):
@@ -241,7 +245,10 @@
     device = column // blocks
     group = device // members
     per_member = chips + blocks + 1
-    place = (group % CORES) * (members * per_member) + (device % members) * per_member + group // CORES
+    owner = device % members
+    here = side_of(lax.axis_index("member"), members)
+    held = (group + side_of(owner, members) + here) % CORES
+    place = held * (members * per_member) + owner * per_member + group // CORES
     rest = jnp.zeros((1, width - blocks * far_count), jnp.int32)
     index_ref[...] = jnp.concatenate([place[b : b + 1, :] for b in range(blocks)] + [rest], axis=1)
     lane = lanes((far_count, width))
@@ -323,7 +330,11 @@
     member = lax.axis_index("member")
     near_count = near_ref.shape[1]
     far_count = coupling_ref.shape[1]
-    fields = [every_ref[pl.ds(core * per_core + m * per_member + chips, blocks), :] for m in range(members)]
+    here = side_of(member, members)
+    fields = []
+    for m in range(members):
+        held = lax.rem(core + side_of(m, members) + here, CORES)
+        fields.append(every_ref[pl.ds(held * per_core + m * per_member + chips, blocks), :])
     choice = near_pick_ref[:, 0 : members * blocks].astype(BF16)
     vector_ref[...] = dot_exact(choice, jnp.concatenate(fields, axis=0), ((1,), (0,)))
     sums = []
@@ -353,14 +364,18 @@
         surface_ref[b : b + 1, :] = near[0:1, b * width : (b + 1) * width] + far + trace_ref[b : b + 1, :]
 
     ends = chips + blocks
-    before = lax.max(member - 1, 0) * per_member + ends
-    after = lax.min(member + 1, members - 1) * per_member + ends
-    inside = jnp.where(member > 0, 1.0, 0.0)
-    mine = every_ref[pl.ds(core * per_core + before, 1), :] * inside
-    theirs = every_ref[pl.ds((1 - core) * per_core + before, 1), :] * inside
-    inside = jnp.where(member + 1 < members, 1.0, 0.0)
-    mine_after = every_ref[pl.ds(core * per_core + after, 1), :] * inside
-    theirs_after = every_ref[pl.ds((1 - core) * per_core + after, 1), :] * inside
+
+    def rim_of(other):
+        inside = jnp.where((other >= 0) & (other < members), 1.0, 0.0)
+        other = lax.clamp(0, other, members - 1)
+        held = lax.rem(core + side_of(other, members) + here, CORES)
+        row = other * per_member + ends
+        mine = every_ref[pl.ds(held * per_core + row, 1), :] * inside
+        theirs = every_ref[pl.ds((1 - held) * per_core + row, 1), :] * inside
+        return mine, theirs
+
+    mine, theirs = rim_of(member - 1)
+    mine_after, theirs_after = rim_of(member + 1)
     shape = (height, width)
     lane = lanes(shape)
     line = rows(shape)
@@ -410,6 +425,11 @@
     near_count = near_columns.shape[1]
     far_count = far_columns.shape[1]
     one_core = [[chip * CORES + core for chip in range(chips)] for core in range(CORES)]
+    crossed = [
+        [(chip * CORES + (core + side_of(m, members)) % CORES) * members + m for m in range(members)]
+        for chip in range(chips)
+        for core in range(CORES)
+    ]
     one_chip = [[chip * CORES + core for core in range(CORES)] for chip in range(chips)]
 
     hbm = pl.BlockSpec(memory_space=pltpu.HBM)
@@ -462,7 +482,12 @@
         compiler_params=PARAMS,
     )(first, rim)
     second = lax.all_to_all(
-        second.reshape(members, 1, per_member * width), "member", split_axis=0, concat_axis=0, tiled=True
+        second.reshape(members, 1, per_member * width),
+        ("group", "member"),
+        split_axis=0,
+        concat_axis=0,
+        axis_index_groups=crossed,
+        tiled=True,
     )
     side = lax.all_gather(side, "group", axis=0, axis_index_groups=one_chip, tiled=True)
     volume, trace, index, keep, near_pick, coupling, left = pl.pallas_call(

time: 55.1 us -> 53.9 us (0.978)
  blocking collectives: 38.9 us -> 33.9 us
  starting transfers between devices: 6.82 us -> 8.73 us
  waiting for transfers between devices: 3.15 us -> 5.03 us
    all_gather x1, blocking collectives: 5.14 us -> 2.1 us  [body(): lax.all_gather(second.reshape(members * per_member, width), 'group', axis...]
    all_gather x1, blocking collectives: 3.94 us -> 1.98 us  [body(): lax.all_gather(side, 'group', axis=0, axis_index_groups=one_chip, tiled=T...]
    all_to_all x1, starting transfers between devices: 6.82 us -> 8.73 us  [body(): lax.all_to_all(second.reshape(members, 1, per_member * width), ('group',...]
    all_to_all x1, waiting for transfers between devices: 3.15 us -> 5.03 us  [body(): lax.all_to_all(second.reshape(members, 1, per_member * width), ('group',...]
where the time goes in v5:
time: 53.9 us; the launch traced here: 53.5 us
  blocking collectives  33.9 us (63%)
  starting transfers between devices  8.73 us (16%)
  Pallas kernels  5.24 us (10%)
  waiting for transfers between devices  5.03 us (9%)
  between operations  0.65 us (1%)
    all_to_all x1, blocking collectives, body(): lax.all_to_all(first.reshape(chips, 1, ROWS * width), 'group', split_axis...  29.8 us
    all_to_all x1, starting transfers between devices, body(): lax.all_to_all(second.reshape(members, 1, per_member * width), ('group',...  8.73 us
    all_to_all x1, waiting for transfers between devices, body(): lax.all_to_all(second.reshape(members, 1, per_member * width), ('group',...  5.03 us
    all_gather x1, blocking collectives, body(): lax.all_gather(second.reshape(members * per_member, width), 'group', axis...  2.1 us
    all_gather x1, blocking collectives, body(): lax.all_gather(side, 'group', axis=0, axis_index_groups=one_chip, tiled=T...  1.98 us
    pallas_call x1, Pallas kernels, body(): pl.pallas_call(functools.partial(local_kernel, members), name='local', ou...  1.78 us
    pallas_call x1, Pallas kernels, body(): pl.pallas_call(pack_kernel, name='pack', out_shape=(out(chips * ROWS, wid...  1.56 us
    pallas_call x1, Pallas kernels, body(): pl.pallas_call(functools.partial(finish_kernel, members, chips), name='fi...  1.13 us
  transfers between devices with their start and end apart: 1, of which 1 were waited for; matrix products, arithmetic and copies ran while one was open for 0% of the time, Pallas kernels for 3%

profile of v5, /device:TPU:1, one launch (start us, length us, event | category | flops | bytes accessed | tf_op | source)
XLA Modules:
  0.0 53.5 jit_solution(10724912720558912317)
XLA Ops:
  0.6 1.6 %pack.1 = (f32[144,128]{1,0:T(8,128)S(1)}, f32[6,128]{1,0:T(8,128)S(1)}) custom-call(f32[2,32,128]{2,1,0:T(8,128)} %edge_in.3, s32[5,1,96]{2,1,0:T(1,128)} %bitcast.14, s32[4,128]{1,0:T(4,128)} %source_in.3, f32[4,128]{1,0:T(4,128)} %surface_in.1, f32[4,32,128]{2,1,0:T(8,128)} %bitcast.13), custom_call_target="tpu_custom_call" | custom-call | tf_op jit(solution)/shard_map/pack/pallas_call | solution.py:450
  2.2 29.8 %all_to_all.10 = f32[48,1,384]{2,1,0:T(1,128)S(1)} all-to-all(f32[48,1,384]{2,1,0:T(1,128)S(1)} %bitcast.10), channel_id=1, replica_groups={{0,16,32,48,64,80,96,112,128,144,160,176,192,208,224,240,256,272,288,30..., dimensions={0} | all-to-all | bytes 147456 | tf_op jit(solution)/shard_map/all_to_all | solution.py:467
  32.0 0.8 %spread.1 = (f32[424,128]{1,0:T(8,128)}, f32[56,128]{1,0:T(8,128)S(1)}) custom-call(f32[144,128]{1,0:T(8,128)S(1)} %bitcast.8, f32[6,128]{1,0:T(8,128)S(1)} %get-tuple-element.14.rim_ref), custom_call_target="tpu_custom_call" | custom-call | tf_op jit(solution)/shard_map/spread/pallas_call | solution.py:475
  32.8 8.7 %all-to-all-start.1 = ((f32[8,1,6784]{2,1,0:T(1,128)}), f32[8,1,6784]{2,1,0:T(1,128)S(1)}, u32[]{:S(2)}, u32[]{:S(2)}) async-start(f32[8,1,6784]{2,1,0:T(1,128)} %bitcast.6), calls=%async_computation.1 | async-start | bytes 434176 | tf_op jit(solution)/shard_map/all_to_all | solution.py:484
  41.5 0.0 copy-start
  41.5 2.0 %all_gather.6 = f32[112,128]{1,0:T(8,128)S(1)} all-gather(f32[56,128]{1,0:T(8,128)S(1)} %get-tuple-element.15), channel_id=1, replica_groups={{0,8},{16,24},{32,40},{48,56},{64,72},{80,88},{96,104},{112,120},{128,1..., dimensions={0}, use_global_device_ids=true | all-gather | bytes 86016 | tf_op jit(solution)/shard_map/all_gather | solution.py:492
  43.5 1.8 %local.1 = (f32[2,32,128]{2,1,0:T(8,128)S(1)}, f32[4,128]{1,0:T(4,128)S(1)}, s32[1,128]{1,0:T(1,128)S(1)}, f32[64,128]{1,0:T(8,128)S(1)}, f32[16,128]{1,0:T(8,12...) custom-call(f32[2,32,128]{2,1,0:T(8,128)} %edge_in.3, f32[2,32,128]{2,1,0:T(8,128)} %conductance_in.1, ...), custom_call_target="tpu_custom_call" | custom-call | flops 10000000 | bytes 2500000 | tf_op jit(solution)/shard_map/local/pallas_call | solution.py:493
  45.3 5.0 %all-to-all-done.1 = f32[8,1,6784]{2,1,0:T(1,128)S(1)} async-done(((f32[8,1,6784]{2,1,0:T(1,128)}), f32[8,1,6784]{2,1,0:T(1,128)S(1)}, u32[]{:S(2)}, u32[]{:S(2)}) %all-to-all-start.1) | async-done | bytes 217120 | tf_op jit(solution)/shard_map/all_to_all | solution.py:484
  50.3 2.1 %all_gather.7.every_ref = f32[848,128]{1,0:T(8,128)S(1)} all-gather(f32[424,128]{1,0:T(8,128)S(1)} %bitcast.11), channel_id=1, replica_groups={{0,8},{16,24},{32,40},{48,56},{64,72},{80,88},{96,104},{112,120},{128,1..., dimensions={0}, use_global_device_ids=true | all-gather | bytes 651264 | tf_op jit(solution)/shard_map/all_gather | solution.py:532
  52.4 0.0 copy-done
  52.4 1.1 %finish.1 = (f32[2,32,128]{2,1,0:T(8,128)}, f32[4,128]{1,0:T(4,128)}) custom-call(f32[2,32,128]{2,1,0:T(8,128)S(1)} %get-tuple-element.16.volume_in, f32[4,128]{1,0:T(4,128)S(1)} %get-tuple-element.17.trace_ref, s32[1,128]{1,0:T(1,128)S(1)} %get-tuple-element.18.index_ref, f32[64,128]{1,0:T(8,128)S(1)} %get-tuple-element.19.keep_ref, ...), custom_call_target="tpu_custom_call" | custom-call | tf_op jit(solution)/shard_map/finish/pallas_call | solution.py:539
Async XLA Ops:
  32.8 17.5 %all-to-all-start.1 = ((f32[8,1,6784]{2,1,0:T(1,128)}), f32[8,1,6784]{2,1,0:T(1,128)S(1)}, u32[]{:S(2)}, u32[]{:S(2)}) async-start(f32[8,1,6784]{2,1,0:T(1,128)} %bitcast.6), calls=%async_computation.1 | async-start | bytes 434176 | tf_op jit(solution)/shard_map/all_to_all | solution.py:484
  41.5 10.9 %copy-start = (f32[4,4,128,128]{3,2,1,0:T(8,128)S(1)}, f32[4,4,128,128]{3,2,1,0:T(8,128)}, u32[]{:S(2)}) copy-start(f32[4,4,128,128]{3,2,1,0:T(8,128)} %near_ref.1) | copy-start | bytes 3145732

commit v6 on v5

--- a/solution.py
+++ b/solution.py
@@ -10,6 +10,8 @@
 F32 = jnp.float32
 BF16 = jnp.bfloat16
 HIGHEST = lax.Precision.HIGHEST
+FIRST_CHIP = 38
+FIRST_MEMBER = 4
 CORES = 2
 ROWS = 3
 SIDE = 8
@@ -46,6 +48,10 @@
 def upright(row, start, shape):
     wide = jnp.where(lanes(shape) == rows(shape) + start, row, 0.0)
     return jnp.sum(wide, axis=1, keepdims=True)
+
+
+def spot(index, first, count):
+    return (index + (count - first % count)) % count
 
 
 def side_of(member, members):
@@ -146,12 +152,15 @@
     out_ref[pl.ds(0, chips, stride=ROWS), :] = jnp.broadcast_to(coeff, (chips, width))
     out_ref[pl.ds(1, chips, stride=ROWS), :] = jnp.broadcast_to(rim, (chips, width))
     tail_ref[...] = tail
+    lane = lanes((chips, width))
     even = tail_ref[pl.ds(0, chips, stride=CORES), :]
     odd = tail_ref[pl.ds(1, chips, stride=CORES), :]
-    lane = lanes((chips, width))
     moved = pltpu.roll(odd, 2 * slots, 1)
     theirs = (lane >= 2 * slots) & (lane < 2 * CORES * slots)
-    out_ref[pl.ds(2, chips, stride=ROWS), :] = jnp.where(theirs, moved, even)
+    both = jnp.where(theirs, moved, even)
+    turn = FIRST_CHIP % chips
+    out_ref[pl.ds(2, chips - turn, stride=ROWS), :] = both[turn:, :]
+    out_ref[pl.ds(2 + ROWS * (chips - turn), turn, stride=ROWS), :] = both[:turn, :]
     rim_ref[0:blocks, :] = surface_ref[...]
     rim_ref[blocks : blocks + 1, :] = ends
     rim_ref[blocks + 1 : blocks + 2, :] = own
@@ -167,8 +176,8 @@
     chip = group // CORES
     before = jnp.where(chip > 0, 1.0, 0.0)
     after = jnp.where(chip + 1 < chips, 1.0, 0.0)
-    chip_before = lax.max(chip - 1, 0) * ROWS
-    chip_after = lax.min(chip + 1, chips - 1) * ROWS
+    chip_before = spot(lax.max(chip - 1, 0), FIRST_CHIP, chips) * ROWS
+    chip_after = spot(lax.min(chip + 1, chips - 1), FIRST_CHIP, chips) * ROWS
     rim_before = first_ref[pl.ds(chip_before + 1, 1), :] * before
     rim_after = first_ref[pl.ds(chip_after + 1, 1), :] * after
     corner_before = first_ref[pl.ds(chip_before + 2, 1), :] * before
@@ -248,7 +257,8 @@
     owner = device % members
     here = side_of(lax.axis_index("member"), members)
     held = (group + side_of(owner, members) + here) % CORES
-    place = held * (members * per_member) + owner * per_member + group // CORES
+    owner = spot(owner, FIRST_MEMBER, members)
+    place = held * (members * per_member) + owner * per_member + spot(group // CORES, FIRST_CHIP, chips)
     rest = jnp.zeros((1, width - blocks * far_count), jnp.int32)
     index_ref[...] = jnp.concatenate([place[b : b + 1, :] for b in range(blocks)] + [rest], axis=1)
     lane = lanes((far_count, width))
@@ -267,7 +277,9 @@
     for c in range(CORES):
         half = side_ref[c, 0:chips, :]
         half = jnp.where(core == 0, half, pltpu.roll(half, width - 2 * slots, 1))
-        tail_ref[pl.ds(c, chips, stride=CORES), :] = half
+        turn = FIRST_CHIP % chips
+        tail_ref[pl.ds(c + CORES * turn, chips - turn, stride=CORES), :] = half[: chips - turn, :]
+        tail_ref[pl.ds(c, turn, stride=CORES), :] = half[chips - turn :, :]
     tail = tail_ref[...]
     slot = rows((groups, width)) * slots
     for b in range(blocks):
@@ -334,7 +346,8 @@
     fields = []
     for m in range(members):
         held = lax.rem(core + side_of(m, members) + here, CORES)
-        fields.append(every_ref[pl.ds(held * per_core + m * per_member + chips, blocks), :])
+        row = held * per_core + spot(m, FIRST_MEMBER, members) * per_member + chips
+        fields.append(every_ref[pl.ds(row, blocks), :])
     choice = near_pick_ref[:, 0 : members * blocks].astype(BF16)
     vector_ref[...] = dot_exact(choice, jnp.concatenate(fields, axis=0), ((1,), (0,)))
     sums = []
@@ -369,7 +382,7 @@
         inside = jnp.where((other >= 0) & (other < members), 1.0, 0.0)
         other = lax.clamp(0, other, members - 1)
         held = lax.rem(core + side_of(other, members) + here, CORES)
-        row = other * per_member + ends
+        row = spot(other, FIRST_MEMBER, members) * per_member + ends
         mine = every_ref[pl.ds(held * per_core + row, 1), :] * inside
         theirs = every_ref[pl.ds((1 - held) * per_core + row, 1), :] * inside
         return mine, theirs
@@ -424,9 +437,11 @@
     left = jnp.swapaxes(basis_left, 1, 2)
     near_count = near_columns.shape[1]
     far_count = far_columns.shape[1]
-    one_core = [[chip * CORES + core for chip in range(chips)] for core in range(CORES)]
+    chip_order = [(FIRST_CHIP + chip) % chips for chip in range(chips)]
+    member_order = [(FIRST_MEMBER + member) % members for member in range(members)]
+    one_core = [[chip * CORES + core for chip in chip_order] for core in range(CORES)]
     crossed = [
-        [(chip * CORES + (core + side_of(m, members)) % CORES) * members + m for m in range(members)]
+        [(chip * CORES + (core + side_of(m, members)) % CORES) * members + m for m in member_order]
         for chip in range(chips)
         for core in range(CORES)
     ]

time: 53.9 us -> 47.3 us (0.88)
  waiting for transfers between devices: 5.03 us -> 0.67 us
  blocking collectives: 33.9 us -> 29.8 us
  starting transfers between devices: 8.73 us -> 10.6 us
    all_to_all x1, waiting for transfers between devices: 5.03 us -> 0.67 us  [body(): lax.all_to_all(second.reshape(members, 1, per_member * width), ('group',...]
    all_to_all x1, blocking collectives: 29.8 us -> 25.8 us  [body(): lax.all_to_all(first.reshape(chips, 1, ROWS * width), 'group', split_axis...]
    all_to_all x1, starting transfers between devices: 8.73 us -> 10.6 us  [body(): lax.all_to_all(second.reshape(members, 1, per_member * width), ('group',...]
  transfers between devices with their start and end apart: 1 -> 1, of which waited for: 1 -> 1; matrix products, arithmetic and copies ran while one was open for 0% -> 0% of each run, Pallas kernels for 3% -> 4%
where the time goes in v6:
time: 47.3 us; the launch traced here: 47 us
  blocking collectives  29.8 us (63%)
  starting transfers between devices  10.6 us (22%)
  Pallas kernels  5.26 us (11%)
  waiting for transfers between devices  0.67 us (1%)
  between operations  0.65 us (1%)
    all_to_all x1, blocking collectives, body(): lax.all_to_all(first.reshape(chips, 1, ROWS * width), 'group', split_axis...  25.8 us
    all_to_all x1, starting transfers between devices, body(): lax.all_to_all(second.reshape(members, 1, per_member * width), ('group',...  10.6 us
    all_gather x1, blocking collectives, body(): lax.all_gather(second.reshape(members * per_member, width), 'group', axis...  2.1 us
    all_gather x1, blocking collectives, body(): lax.all_gather(side, 'group', axis=0, axis_index_groups=one_chip, tiled=T...  1.96 us
    pallas_call x1, Pallas kernels, body(): pl.pallas_call(functools.partial(local_kernel, members), name='local', ou...  1.78 us
    pallas_call x1, Pallas kernels, body(): pl.pallas_call(pack_kernel, name='pack', out_shape=(out(chips * ROWS, wid...  1.56 us
    pallas_call x1, Pallas kernels, body(): pl.pallas_call(functools.partial(finish_kernel, members, chips), name='fi...  1.13 us
  transfers between devices with their start and end apart: 1, of which 1 were waited for; matrix products, arithmetic and copies ran while one was open for 0% of the time, Pallas kernels for 4%

profile of v6, /device:TPU:1, one launch (start us, length us, event | category | flops | bytes accessed | tf_op | source)
XLA Modules:
  0.0 47.0 jit_solution(6857419554072147859)
XLA Ops:
  0.6 1.6 %pack.1 = (f32[144,128]{1,0:T(8,128)S(1)}, f32[6,128]{1,0:T(8,128)S(1)}) custom-call(f32[2,32,128]{2,1,0:T(8,128)} %edge_in.3, s32[5,1,96]{2,1,0:T(1,128)} %bitcast.14, s32[4,128]{1,0:T(4,128)} %source_in.3, f32[4,128]{1,0:T(4,128)} %surface_in.1, f32[4,32,128]{2,1,0:T(8,128)} %bitcast.13), custom_call_target="tpu_custom_call" | custom-call | tf_op jit(solution)/shard_map/pack/pallas_call | solution.py:465
  2.2 25.8 %all_to_all.10 = f32[48,1,384]{2,1,0:T(1,128)S(1)} all-to-all(f32[48,1,384]{2,1,0:T(1,128)S(1)} %bitcast.10), channel_id=1, replica_groups={{608,624,640,656,672,688,704,720,736,752,0,16,32,48,64,80,96,112,128,14..., dimensions={0} | all-to-all | bytes 147456 | tf_op jit(solution)/shard_map/all_to_all | solution.py:482
  28.0 0.8 %spread.1 = (f32[424,128]{1,0:T(8,128)}, f32[56,128]{1,0:T(8,128)S(1)}) custom-call(f32[144,128]{1,0:T(8,128)S(1)} %bitcast.8, f32[6,128]{1,0:T(8,128)S(1)} %get-tuple-element.14.rim_ref), custom_call_target="tpu_custom_call" | custom-call | tf_op jit(solution)/shard_map/spread/pallas_call | solution.py:490
  28.8 10.6 %all-to-all-start.1 = ((f32[8,1,6784]{2,1,0:T(1,128)}), f32[8,1,6784]{2,1,0:T(1,128)S(1)}, u32[]{:S(2)}, u32[]{:S(2)}) async-start(f32[8,1,6784]{2,1,0:T(1,128)} %bitcast.6), calls=%async_computation.1 | async-start | bytes 434176 | tf_op jit(solution)/shard_map/all_to_all | solution.py:499
  39.3 0.0 copy-start
  39.3 2.0 %all_gather.6 = f32[112,128]{1,0:T(8,128)S(1)} all-gather(f32[56,128]{1,0:T(8,128)S(1)} %get-tuple-element.15), channel_id=1, replica_groups={{0,8},{16,24},{32,40},{48,56},{64,72},{80,88},{96,104},{112,120},{128,1..., dimensions={0}, use_global_device_ids=true | all-gather | bytes 86016 | tf_op jit(solution)/shard_map/all_gather | solution.py:507
  41.3 1.8 %local.1 = (f32[2,32,128]{2,1,0:T(8,128)S(1)}, f32[4,128]{1,0:T(4,128)S(1)}, s32[1,128]{1,0:T(1,128)S(1)}, f32[64,128]{1,0:T(8,128)S(1)}, f32[16,128]{1,0:T(8,12...) custom-call(f32[2,32,128]{2,1,0:T(8,128)} %edge_in.3, f32[2,32,128]{2,1,0:T(8,128)} %conductance_in.1, ...), custom_call_target="tpu_custom_call" | custom-call | flops 10000000 | bytes 2500000 | tf_op jit(solution)/shard_map/local/pallas_call | solution.py:508
  43.1 0.7 %all-to-all-done.1 = f32[8,1,6784]{2,1,0:T(1,128)S(1)} async-done(((f32[8,1,6784]{2,1,0:T(1,128)}), f32[8,1,6784]{2,1,0:T(1,128)S(1)}, u32[]{:S(2)}, u32[]{:S(2)}) %all-to-all-start.1) | async-done | bytes 217120 | tf_op jit(solution)/shard_map/all_to_all | solution.py:499
  43.8 2.1 %all_gather.7.every_ref = f32[848,128]{1,0:T(8,128)S(1)} all-gather(f32[424,128]{1,0:T(8,128)S(1)} %bitcast.11), channel_id=1, replica_groups={{0,8},{16,24},{32,40},{48,56},{64,72},{80,88},{96,104},{112,120},{128,1..., dimensions={0}, use_global_device_ids=true | all-gather | bytes 651264 | tf_op jit(solution)/shard_map/all_gather | solution.py:547
  45.9 0.0 copy-done
  45.9 1.1 %finish.1 = (f32[2,32,128]{2,1,0:T(8,128)}, f32[4,128]{1,0:T(4,128)}) custom-call(f32[2,32,128]{2,1,0:T(8,128)S(1)} %get-tuple-element.16.volume_in, f32[4,128]{1,0:T(4,128)S(1)} %get-tuple-element.17.trace_ref, s32[1,128]{1,0:T(1,128)S(1)} %get-tuple-element.18.index_ref, f32[64,128]{1,0:T(8,128)S(1)} %get-tuple-element.19.keep_ref, ...), custom_call_target="tpu_custom_call" | custom-call | tf_op jit(solution)/shard_map/finish/pallas_call | solution.py:554
Async XLA Ops:
  28.8 15.0 %all-to-all-start.1 = ((f32[8,1,6784]{2,1,0:T(1,128)}), f32[8,1,6784]{2,1,0:T(1,128)S(1)}, u32[]{:S(2)}, u32[]{:S(2)}) async-start(f32[8,1,6784]{2,1,0:T(1,128)} %bitcast.6), calls=%async_computation.1 | async-start | bytes 434176 | tf_op jit(solution)/shard_map/all_to_all | solution.py:499
  39.3 6.5 %copy-start = (f32[4,4,128,128]{3,2,1,0:T(8,128)S(1)}, f32[4,4,128,128]{3,2,1,0:T(8,128)}, u32[]{:S(2)}) copy-start(f32[4,4,128,128]{3,2,1,0:T(8,128)} %near_ref.1) | copy-start | bytes 3145732

commit v7 on v6

--- a/solution.py
+++ b/solution.py
@@ -10,7 +10,7 @@
 F32 = jnp.float32
 BF16 = jnp.bfloat16
 HIGHEST = lax.Precision.HIGHEST
-FIRST_CHIP = 38
+FIRST_CHIP = 34
 FIRST_MEMBER = 4
 CORES = 2
 ROWS = 3
@@ -127,19 +127,22 @@
         ],
         axis=1,
     )
-    index = slot_columns(send_ref)
     parts = split3(edge_ref[...].reshape(2 * height, width))
-    lane = lanes((groups, width))
-    tail = jnp.where(lane == 2 * CORES * slots, last_x[0:1, 0:1], 0.0)
+    tall = (2 * height, groups)
+    values = []
     for s in range(slots):
-        column = jnp.broadcast_to(index[:, s : s + 1], (groups, width))
-        choice = (lanes((groups, 2 * height)) == (column >> bits)[:, 0 : 2 * height]).astype(BF16)
+        index = send_ref[s]
+        choice = (rows(tall) == (index >> bits)).astype(BF16)
         picked = None
         for part in parts:
-            term = lax.dot_general(choice, part, (((1,), (0,)), ((), ())), preferred_element_type=F32)
+            term = lax.dot_general(part, choice, (((0,), (0,)), ((), ())), preferred_element_type=F32)
             picked = term if picked is None else picked + term
-        value = jnp.sum(jnp.where(lane == (column & (width - 1)), picked, 0.0), axis=1, keepdims=True)
-        tail = jnp.where(lane == s, value, tail)
+        here = rows((width, groups)) == (index & (width - 1))
+        values.append(jnp.sum(jnp.where(here, picked, 0.0), axis=0, keepdims=True))
+    values = jnp.concatenate(values + [jnp.zeros((8 - slots, groups), F32)], axis=0).T
+    lane = lanes((groups, width))
+    tail = jnp.concatenate([values, jnp.zeros((groups, width - 8), F32)], axis=1)
+    tail = jnp.where(lane == 2 * CORES * slots, last_x[0:1, 0:1], tail)
     slot = rows((groups, width)) * slots
     for s in range(slots):
         total = jnp.zeros((groups, width), F32)

time: 47.3 us -> 47.4 us (level)
  no operation moved by 1% of the time
where the time goes in v7:
time: 47.4 us; the launch traced here: 47.1 us
  blocking collectives  29.9 us (63%)
  starting transfers between devices  10.5 us (22%)
  Pallas kernels  5.2 us (11%)
  waiting for transfers between devices  0.72 us (2%)
  between operations  0.65 us (1%)
    all_to_all x1, blocking collectives, body(): lax.all_to_all(first.reshape(chips, 1, ROWS * width), 'group', split_axis...  25.9 us
    all_to_all x1, starting transfers between devices, body(): lax.all_to_all(second.reshape(members, 1, per_member * width), ('group',...  10.5 us
    all_gather x1, blocking collectives, body(): lax.all_gather(second.reshape(members * per_member, width), 'group', axis...  2.1 us
    all_gather x1, blocking collectives, body(): lax.all_gather(side, 'group', axis=0, axis_index_groups=one_chip, tiled=T...  1.96 us
    pallas_call x1, Pallas kernels, body(): pl.pallas_call(functools.partial(local_kernel, members), name='local', ou...  1.78 us
    pallas_call x1, Pallas kernels, body(): pl.pallas_call(pack_kernel, name='pack', out_shape=(out(chips * ROWS, wid...  1.51 us
    pallas_call x1, Pallas kernels, body(): pl.pallas_call(functools.partial(finish_kernel, members, chips), name='fi...  1.13 us
  transfers between devices with their start and end apart: 1, of which 1 were waited for; matrix products, arithmetic and copies ran while one was open for 0% of the time, Pallas kernels for 4%

profile of v7, /device:TPU:1, one launch (start us, length us, event | category | flops | bytes accessed | tf_op | source)
XLA Modules:
  0.0 47.1 jit_solution(5978989952451758885)
XLA Ops:
  0.6 1.5 %pack.1 = (f32[144,128]{1,0:T(8,128)S(1)}, f32[6,128]{1,0:T(8,128)S(1)}) custom-call(f32[2,32,128]{2,1,0:T(8,128)} %edge_in.3, s32[5,1,96]{2,1,0:T(1,128)} %bitcast.14, s32[4,128]{1,0:T(4,128)} %source_in.3, f32[4,128]{1,0:T(4,128)} %surface_in.1, f32[4,32,128]{2,1,0:T(8,128)} %bitcast.13), custom_call_target="tpu_custom_call" | custom-call | tf_op jit(solution)/shard_map/pack/pallas_call | solution.py:468
  2.2 25.9 %all_to_all.10 = f32[48,1,384]{2,1,0:T(1,128)S(1)} all-to-all(f32[48,1,384]{2,1,0:T(1,128)S(1)} %bitcast.10), channel_id=1, replica_groups={{544,560,576,592,608,624,640,656,672,688,704,720,736,752,0,16,32,48,64,..., dimensions={0} | all-to-all | bytes 147456 | tf_op jit(solution)/shard_map/all_to_all | solution.py:485
  28.0 0.8 %spread.1 = (f32[424,128]{1,0:T(8,128)}, f32[56,128]{1,0:T(8,128)S(1)}) custom-call(f32[144,128]{1,0:T(8,128)S(1)} %bitcast.8, f32[6,128]{1,0:T(8,128)S(1)} %get-tuple-element.14.rim_ref), custom_call_target="tpu_custom_call" | custom-call | tf_op jit(solution)/shard_map/spread/pallas_call | solution.py:493
  28.8 10.5 %all-to-all-start.1 = ((f32[8,1,6784]{2,1,0:T(1,128)}), f32[8,1,6784]{2,1,0:T(1,128)S(1)}, u32[]{:S(2)}, u32[]{:S(2)}) async-start(f32[8,1,6784]{2,1,0:T(1,128)} %bitcast.6), calls=%async_computation.1 | async-start | bytes 434176 | tf_op jit(solution)/shard_map/all_to_all | solution.py:502
  39.3 0.0 copy-start
  39.3 2.0 %all_gather.6 = f32[112,128]{1,0:T(8,128)S(1)} all-gather(f32[56,128]{1,0:T(8,128)S(1)} %get-tuple-element.15), channel_id=1, replica_groups={{0,8},{16,24},{32,40},{48,56},{64,72},{80,88},{96,104},{112,120},{128,1..., dimensions={0}, use_global_device_ids=true | all-gather | bytes 86016 | tf_op jit(solution)/shard_map/all_gather | solution.py:510
  41.3 1.8 %local.1 = (f32[2,32,128]{2,1,0:T(8,128)S(1)}, f32[4,128]{1,0:T(4,128)S(1)}, s32[1,128]{1,0:T(1,128)S(1)}, f32[64,128]{1,0:T(8,128)S(1)}, f32[16,128]{1,0:T(8,12...) custom-call(f32[2,32,128]{2,1,0:T(8,128)} %edge_in.3, f32[2,32,128]{2,1,0:T(8,128)} %conductance_in.1, ...), custom_call_target="tpu_custom_call" | custom-call | flops 10000000 | bytes 2500000 | tf_op jit(solution)/shard_map/local/pallas_call | solution.py:511
  43.1 0.7 %all-to-all-done.1 = f32[8,1,6784]{2,1,0:T(1,128)S(1)} async-done(((f32[8,1,6784]{2,1,0:T(1,128)}), f32[8,1,6784]{2,1,0:T(1,128)S(1)}, u32[]{:S(2)}, u32[]{:S(2)}) %all-to-all-start.1) | async-done | bytes 217120 | tf_op jit(solution)/shard_map/all_to_all | solution.py:502
  43.8 2.1 %all_gather.7.every_ref = f32[848,128]{1,0:T(8,128)S(1)} all-gather(f32[424,128]{1,0:T(8,128)S(1)} %bitcast.11), channel_id=1, replica_groups={{0,8},{16,24},{32,40},{48,56},{64,72},{80,88},{96,104},{112,120},{128,1..., dimensions={0}, use_global_device_ids=true | all-gather | bytes 651264 | tf_op jit(solution)/shard_map/all_gather | solution.py:550
  45.9 0.0 copy-done
  45.9 1.1 %finish.1 = (f32[2,32,128]{2,1,0:T(8,128)}, f32[4,128]{1,0:T(4,128)}) custom-call(f32[2,32,128]{2,1,0:T(8,128)S(1)} %get-tuple-element.16.volume_in, f32[4,128]{1,0:T(4,128)S(1)} %get-tuple-element.17.trace_ref, s32[1,128]{1,0:T(1,128)S(1)} %get-tuple-element.18.index_ref, f32[64,128]{1,0:T(8,128)S(1)} %get-tuple-element.19.keep_ref, ...), custom_call_target="tpu_custom_call" | custom-call | tf_op jit(solution)/shard_map/finish/pallas_call | solution.py:557
Async XLA Ops:
  28.8 15.0 %all-to-all-start.1 = ((f32[8,1,6784]{2,1,0:T(1,128)}), f32[8,1,6784]{2,1,0:T(1,128)S(1)}, u32[]{:S(2)}, u32[]{:S(2)}) async-start(f32[8,1,6784]{2,1,0:T(1,128)} %bitcast.6), calls=%async_computation.1 | async-start | bytes 434176 | tf_op jit(solution)/shard_map/all_to_all | solution.py:502
  39.3 6.6 %copy-start = (f32[4,4,128,128]{3,2,1,0:T(8,128)S(1)}, f32[4,4,128,128]{3,2,1,0:T(8,128)}, u32[]{:S(2)}) copy-start(f32[4,4,128,128]{3,2,1,0:T(8,128)} %near_ref.1) | copy-start | bytes 3145732

commit v8 on v6

--- a/solution.py
+++ b/solution.py
@@ -256,7 +256,7 @@
     per_member = chips + blocks + 1
     owner = device % members
     here = side_of(lax.axis_index("member"), members)
-    held = (group + side_of(owner, members) + here) % CORES
+    held = (group + side_of(owner, members) + here + 1) % CORES
     owner = spot(owner, FIRST_MEMBER, members)
     place = held * (members * per_member) + owner * per_member + spot(group // CORES, FIRST_CHIP, chips)
     rest = jnp.zeros((1, width - blocks * far_count), jnp.int32)
@@ -275,7 +275,7 @@
         picked = jnp.sum(picked, axis=1, keepdims=True).astype(jnp.int32)
         near_pick_ref[b * near_count : (b + 1) * near_count, :] = (lanes((near_count, width)) == picked).astype(F32)
     for c in range(CORES):
-        half = side_ref[c, 0:chips, :]
+        half = side_ref[CORES - 1 - c, 0:chips, :]
         half = jnp.where(core == 0, half, pltpu.roll(half, width - 2 * slots, 1))
         turn = FIRST_CHIP % chips
         tail_ref[pl.ds(c + CORES * turn, chips - turn, stride=CORES), :] = half[: chips - turn, :]
@@ -301,8 +301,8 @@
     shape = (height, width)
     lane = lanes(shape)
     line = rows(shape)
-    own = side_ref[1 - core, chips : chips + 1, :]
-    other = side_ref[1 - core, chips + SIDE // 2 : chips + SIDE // 2 + 1, :]
+    own = side_ref[core, chips : chips + 1, :]
+    other = side_ref[core, chips + SIDE // 2 : chips + SIDE // 2 + 1, :]
     above = jnp.where(core == 0, other, own)
     below = jnp.where(core == 0, own, other)
     next_x = jnp.where(lane == width - 1, 0.0, pltpu.roll(edge_x, width - 1, 1))
@@ -345,7 +345,7 @@
     here = side_of(member, members)
     fields = []
     for m in range(members):
-        held = lax.rem(core + side_of(m, members) + here, CORES)
+        held = lax.rem(core + side_of(m, members) + here + 1, CORES)
         row = held * per_core + spot(m, FIRST_MEMBER, members) * per_member + chips
         fields.append(every_ref[pl.ds(row, blocks), :])
     choice = near_pick_ref[:, 0 : members * blocks].astype(BF16)
@@ -381,7 +381,7 @@
     def rim_of(other):
         inside = jnp.where((other >= 0) & (other < members), 1.0, 0.0)
         other = lax.clamp(0, other, members - 1)
-        held = lax.rem(core + side_of(other, members) + here, CORES)
+        held = lax.rem(core + side_of(other, members) + here + 1, CORES)
         row = spot(other, FIRST_MEMBER, members) * per_member + ends
         mine = every_ref[pl.ds(held * per_core + row, 1), :] * inside
         theirs = every_ref[pl.ds((1 - held) * per_core + row, 1), :] * inside
@@ -445,7 +445,7 @@
         for chip in range(chips)
         for core in range(CORES)
     ]
-    one_chip = [[chip * CORES + core for core in range(CORES)] for chip in range(chips)]
+    one_chip = [[chip * CORES + core for core in reversed(range(CORES))] for chip in range(chips)]
 
     hbm = pl.BlockSpec(memory_space=pltpu.HBM)
     edge_field, conductance, send, panel_source, surface_field, right, left, far_coupling = [

time: 47.3 us -> 47.3 us (level)
  no operation moved by 1% of the time
where the time goes in v8:
time: 47.3 us; the launch traced here: 47 us
  blocking collectives  29.8 us (63%)
  starting transfers between devices  10.6 us (22%)
  Pallas kernels  5.26 us (11%)
  waiting for transfers between devices  0.67 us (1%)
  between operations  0.65 us (1%)
    all_to_all x1, blocking collectives, body(): lax.all_to_all(first.reshape(chips, 1, ROWS * width), 'group', split_axis...  25.8 us
    all_to_all x1, starting transfers between devices, body(): lax.all_to_all(second.reshape(members, 1, per_member * width), ('group',...  10.6 us
    all_gather x1, blocking collectives, body(): lax.all_gather(second.reshape(members * per_member, width), 'group', axis...  2.1 us
    all_gather x1, blocking collectives, body(): lax.all_gather(side, 'group', axis=0, axis_index_groups=one_chip, tiled=T...  1.96 us
    pallas_call x1, Pallas kernels, body(): pl.pallas_call(functools.partial(local_kernel, members), name='local', ou...  1.78 us
    pallas_call x1, Pallas kernels, body(): pl.pallas_call(pack_kernel, name='pack', out_shape=(out(chips * ROWS, wid...  1.56 us
    pallas_call x1, Pallas kernels, body(): pl.pallas_call(functools.partial(finish_kernel, members, chips), name='fi...  1.13 us
  transfers between devices with their start and end apart: 1, of which 1 were waited for; matrix products, arithmetic and copies ran while one was open for 0% of the time, Pallas kernels for 4%

profile of v8, /device:TPU:1, one launch (start us, length us, event | category | flops | bytes accessed | tf_op | source)
XLA Modules:
  0.0 47.0 jit_solution(6127022520349098249)
XLA Ops:
  0.6 1.6 %pack.1 = (f32[144,128]{1,0:T(8,128)S(1)}, f32[6,128]{1,0:T(8,128)S(1)}) custom-call(f32[2,32,128]{2,1,0:T(8,128)} %edge_in.3, s32[5,1,96]{2,1,0:T(1,128)} %bitcast.14, s32[4,128]{1,0:T(4,128)} %source_in.3, f32[4,128]{1,0:T(4,128)} %surface_in.1, f32[4,32,128]{2,1,0:T(8,128)} %bitcast.13), custom_call_target="tpu_custom_call" | custom-call | tf_op jit(solution)/shard_map/pack/pallas_call | solution.py:465
  2.2 25.8 %all_to_all.10 = f32[48,1,384]{2,1,0:T(1,128)S(1)} all-to-all(f32[48,1,384]{2,1,0:T(1,128)S(1)} %bitcast.10), channel_id=1, replica_groups={{608,624,640,656,672,688,704,720,736,752,0,16,32,48,64,80,96,112,128,14..., dimensions={0} | all-to-all | bytes 147456 | tf_op jit(solution)/shard_map/all_to_all | solution.py:482
  28.0 0.8 %spread.1 = (f32[424,128]{1,0:T(8,128)}, f32[56,128]{1,0:T(8,128)S(1)}) custom-call(f32[144,128]{1,0:T(8,128)S(1)} %bitcast.8, f32[6,128]{1,0:T(8,128)S(1)} %get-tuple-element.14.rim_ref), custom_call_target="tpu_custom_call" | custom-call | tf_op jit(solution)/shard_map/spread/pallas_call | solution.py:490
  28.8 10.6 %all-to-all-start.1 = ((f32[8,1,6784]{2,1,0:T(1,128)}), f32[8,1,6784]{2,1,0:T(1,128)S(1)}, u32[]{:S(2)}, u32[]{:S(2)}) async-start(f32[8,1,6784]{2,1,0:T(1,128)} %bitcast.6), calls=%async_computation.1 | async-start | bytes 434176 | tf_op jit(solution)/shard_map/all_to_all | solution.py:499
  39.3 0.0 copy-start
  39.3 2.0 %all_gather.6 = f32[112,128]{1,0:T(8,128)S(1)} all-gather(f32[56,128]{1,0:T(8,128)S(1)} %get-tuple-element.15), channel_id=1, replica_groups={{8,0},{24,16},{40,32},{56,48},{72,64},{88,80},{104,96},{120,112},{136,1..., dimensions={0}, use_global_device_ids=true | all-gather | bytes 86016 | tf_op jit(solution)/shard_map/all_gather | solution.py:507
  41.3 1.8 %local.1 = (f32[2,32,128]{2,1,0:T(8,128)S(1)}, f32[4,128]{1,0:T(4,128)S(1)}, s32[1,128]{1,0:T(1,128)S(1)}, f32[64,128]{1,0:T(8,128)S(1)}, f32[16,128]{1,0:T(8,12...) custom-call(f32[2,32,128]{2,1,0:T(8,128)} %edge_in.3, f32[2,32,128]{2,1,0:T(8,128)} %conductance_in.1, ...), custom_call_target="tpu_custom_call" | custom-call | flops 10000000 | bytes 2500000 | tf_op jit(solution)/shard_map/local/pallas_call | solution.py:508
  43.1 0.7 %all-to-all-done.1 = f32[8,1,6784]{2,1,0:T(1,128)S(1)} async-done(((f32[8,1,6784]{2,1,0:T(1,128)}), f32[8,1,6784]{2,1,0:T(1,128)S(1)}, u32[]{:S(2)}, u32[]{:S(2)}) %all-to-all-start.1) | async-done | bytes 217120 | tf_op jit(solution)/shard_map/all_to_all | solution.py:499
  43.8 2.1 %all_gather.7.every_ref = f32[848,128]{1,0:T(8,128)S(1)} all-gather(f32[424,128]{1,0:T(8,128)S(1)} %bitcast.11), channel_id=1, replica_groups={{8,0},{24,16},{40,32},{56,48},{72,64},{88,80},{104,96},{120,112},{136,1..., dimensions={0}, use_global_device_ids=true | all-gather | bytes 651264 | tf_op jit(solution)/shard_map/all_gather | solution.py:547
  45.9 0.0 copy-done
  45.9 1.1 %finish.1 = (f32[2,32,128]{2,1,0:T(8,128)}, f32[4,128]{1,0:T(4,128)}) custom-call(f32[2,32,128]{2,1,0:T(8,128)S(1)} %get-tuple-element.16.volume_in, f32[4,128]{1,0:T(4,128)S(1)} %get-tuple-element.17.trace_ref, s32[1,128]{1,0:T(1,128)S(1)} %get-tuple-element.18.index_ref, f32[64,128]{1,0:T(8,128)S(1)} %get-tuple-element.19.keep_ref, ...), custom_call_target="tpu_custom_call" | custom-call | tf_op jit(solution)/shard_map/finish/pallas_call | solution.py:554
Async XLA Ops:
  28.8 15.0 %all-to-all-start.1 = ((f32[8,1,6784]{2,1,0:T(1,128)}), f32[8,1,6784]{2,1,0:T(1,128)S(1)}, u32[]{:S(2)}, u32[]{:S(2)}) async-start(f32[8,1,6784]{2,1,0:T(1,128)} %bitcast.6), calls=%async_computation.1 | async-start | bytes 434176 | tf_op jit(solution)/shard_map/all_to_all | solution.py:499
  39.3 6.5 %copy-start = (f32[4,4,128,128]{3,2,1,0:T(8,128)S(1)}, f32[4,4,128,128]{3,2,1,0:T(8,128)}, u32[]{:S(2)}) copy-start(f32[4,4,128,128]{3,2,1,0:T(8,128)} %near_ref.1) | copy-start | bytes 3145732

commit v9 on v6

--- a/solution.py
+++ b/solution.py
@@ -10,7 +10,7 @@
 F32 = jnp.float32
 BF16 = jnp.bfloat16
 HIGHEST = lax.Precision.HIGHEST
-FIRST_CHIP = 38
+FIRST_CHIP = 34
 FIRST_MEMBER = 4
 CORES = 2
 ROWS = 3

time: 47.3 us -> 47.4 us (level)
  no operation moved by 1% of the time
where the time goes in v9:
time: 47.4 us; the launch traced here: 47.1 us
  blocking collectives  29.9 us (63%)
  starting transfers between devices  10.5 us (22%)
  Pallas kernels  5.25 us (11%)
  waiting for transfers between devices  0.72 us (2%)
  between operations  0.65 us (1%)
    all_to_all x1, blocking collectives, body(): lax.all_to_all(first.reshape(chips, 1, ROWS * width), 'group', split_axis...  25.9 us
    all_to_all x1, starting transfers between devices, body(): lax.all_to_all(second.reshape(members, 1, per_member * width), ('group',...  10.5 us
    all_gather x1, blocking collectives, body(): lax.all_gather(second.reshape(members * per_member, width), 'group', axis...  2.1 us
    all_gather x1, blocking collectives, body(): lax.all_gather(side, 'group', axis=0, axis_index_groups=one_chip, tiled=T...  1.96 us
    pallas_call x1, Pallas kernels, body(): pl.pallas_call(functools.partial(local_kernel, members), name='local', ou...  1.78 us
    pallas_call x1, Pallas kernels, body(): pl.pallas_call(pack_kernel, name='pack', out_shape=(out(chips * ROWS, wid...  1.56 us
    pallas_call x1, Pallas kernels, body(): pl.pallas_call(functools.partial(finish_kernel, members, chips), name='fi...  1.13 us
  transfers between devices with their start and end apart: 1, of which 1 were waited for; matrix products, arithmetic and copies ran while one was open for 0% of the time, Pallas kernels for 4%

profile of v9, /device:TPU:1, one launch (start us, length us, event | category | flops | bytes accessed | tf_op | source)
XLA Modules:
  0.0 47.1 jit_solution(6684827277602120465)
XLA Ops:
  0.6 1.6 %pack.1 = (f32[144,128]{1,0:T(8,128)S(1)}, f32[6,128]{1,0:T(8,128)S(1)}) custom-call(f32[2,32,128]{2,1,0:T(8,128)} %edge_in.3, s32[5,1,96]{2,1,0:T(1,128)} %bitcast.14, s32[4,128]{1,0:T(4,128)} %source_in.3, f32[4,128]{1,0:T(4,128)} %surface_in.1, f32[4,32,128]{2,1,0:T(8,128)} %bitcast.13), custom_call_target="tpu_custom_call" | custom-call | tf_op jit(solution)/shard_map/pack/pallas_call | solution.py:465
  2.2 25.9 %all_to_all.10 = f32[48,1,384]{2,1,0:T(1,128)S(1)} all-to-all(f32[48,1,384]{2,1,0:T(1,128)S(1)} %bitcast.10), channel_id=1, replica_groups={{544,560,576,592,608,624,640,656,672,688,704,720,736,752,0,16,32,48,64,..., dimensions={0} | all-to-all | bytes 147456 | tf_op jit(solution)/shard_map/all_to_all | solution.py:482
  28.1 0.8 %spread.1 = (f32[424,128]{1,0:T(8,128)}, f32[56,128]{1,0:T(8,128)S(1)}) custom-call(f32[144,128]{1,0:T(8,128)S(1)} %bitcast.8, f32[6,128]{1,0:T(8,128)S(1)} %get-tuple-element.14.rim_ref), custom_call_target="tpu_custom_call" | custom-call | tf_op jit(solution)/shard_map/spread/pallas_call | solution.py:490
  28.9 10.5 %all-to-all-start.1 = ((f32[8,1,6784]{2,1,0:T(1,128)}), f32[8,1,6784]{2,1,0:T(1,128)S(1)}, u32[]{:S(2)}, u32[]{:S(2)}) async-start(f32[8,1,6784]{2,1,0:T(1,128)} %bitcast.6), calls=%async_computation.1 | async-start | bytes 434176 | tf_op jit(solution)/shard_map/all_to_all | solution.py:499
  39.4 0.0 copy-start
  39.4 2.0 %all_gather.6 = f32[112,128]{1,0:T(8,128)S(1)} all-gather(f32[56,128]{1,0:T(8,128)S(1)} %get-tuple-element.15), channel_id=1, replica_groups={{0,8},{16,24},{32,40},{48,56},{64,72},{80,88},{96,104},{112,120},{128,1..., dimensions={0}, use_global_device_ids=true | all-gather | bytes 86016 | tf_op jit(solution)/shard_map/all_gather | solution.py:507
  41.4 1.8 %local.1 = (f32[2,32,128]{2,1,0:T(8,128)S(1)}, f32[4,128]{1,0:T(4,128)S(1)}, s32[1,128]{1,0:T(1,128)S(1)}, f32[64,128]{1,0:T(8,128)S(1)}, f32[16,128]{1,0:T(8,12...) custom-call(f32[2,32,128]{2,1,0:T(8,128)} %edge_in.3, f32[2,32,128]{2,1,0:T(8,128)} %conductance_in.1, ...), custom_call_target="tpu_custom_call" | custom-call | flops 10000000 | bytes 2500000 | tf_op jit(solution)/shard_map/local/pallas_call | solution.py:508
  43.1 0.7 %all-to-all-done.1 = f32[8,1,6784]{2,1,0:T(1,128)S(1)} async-done(((f32[8,1,6784]{2,1,0:T(1,128)}), f32[8,1,6784]{2,1,0:T(1,128)S(1)}, u32[]{:S(2)}, u32[]{:S(2)}) %all-to-all-start.1) | async-done | bytes 217120 | tf_op jit(solution)/shard_map/all_to_all | solution.py:499
  43.9 2.1 %all_gather.7.every_ref = f32[848,128]{1,0:T(8,128)S(1)} all-gather(f32[424,128]{1,0:T(8,128)S(1)} %bitcast.11), channel_id=1, replica_groups={{0,8},{16,24},{32,40},{48,56},{64,72},{80,88},{96,104},{112,120},{128,1..., dimensions={0}, use_global_device_ids=true | all-gather | bytes 651264 | tf_op jit(solution)/shard_map/all_gather | solution.py:547
  46.0 0.0 copy-done
  46.0 1.1 %finish.1 = (f32[2,32,128]{2,1,0:T(8,128)}, f32[4,128]{1,0:T(4,128)}) custom-call(f32[2,32,128]{2,1,0:T(8,128)S(1)} %get-tuple-element.16.volume_in, f32[4,128]{1,0:T(4,128)S(1)} %get-tuple-element.17.trace_ref, s32[1,128]{1,0:T(1,128)S(1)} %get-tuple-element.18.index_ref, f32[64,128]{1,0:T(8,128)S(1)} %get-tuple-element.19.keep_ref, ...), custom_call_target="tpu_custom_call" | custom-call | tf_op jit(solution)/shard_map/finish/pallas_call | solution.py:554
Async XLA Ops:
  28.9 15.0 %all-to-all-start.1 = ((f32[8,1,6784]{2,1,0:T(1,128)}), f32[8,1,6784]{2,1,0:T(1,128)S(1)}, u32[]{:S(2)}, u32[]{:S(2)}) async-start(f32[8,1,6784]{2,1,0:T(1,128)} %bitcast.6), calls=%async_computation.1 | async-start | bytes 434176 | tf_op jit(solution)/shard_map/all_to_all | solution.py:499
  39.4 6.6 %copy-start = (f32[4,4,128,128]{3,2,1,0:T(8,128)S(1)}, f32[4,4,128,128]{3,2,1,0:T(8,128)}, u32[]{:S(2)}) copy-start(f32[4,4,128,128]{3,2,1,0:T(8,128)} %near_ref.1) | copy-start | bytes 3145732
